TPU v7x, 32 devices: a whole 2x2x4 slice. The times are simulated.
32 devices in a mesh: groups: 2 (over y), tm: 4 (over z), band: 2 (over x), tmpl: 2 (over core).
Axes of the slice: x: 2, y: 2, z: 4, core: 2. Of those that a mesh axis runs over, the one named last changes fastest.
Arguments:
- sft_bins: float32 [2, 128, 2048], P(None, ('groups', 'tm'), 'band'), parts along dimension 1, may hold values from -6 to 6
- delay_code: int32 [8, 128, 1024], P(('groups', 'tmpl'), None, ('tm', 'band')), parts along dimension 0, may hold values from 0 to 16007, as said below
- antenna: float32 [8, 2, 128, 1024], P(('groups', 'tmpl'), None, None, ('tm', 'band')), parts along dimension 0, may hold values from -10 to 10
Outputs:
- f_stat: float32 [8, 128, 8, 128], P(('groups', 'tmpl'), None, ('tm', 'band')), parts along dimension 0
There are 2 independent parts, one for each index of `groups`. A program takes and returns all parts, laid end to end along the dimension named above; each array names one. Nothing has to cross between parts.
Inputs may be any that keep to these rules, and one draw needn't show every extreme that they name: `delay_code`: the whole delay o of a template is the same for all samples n of each aligned run of 256 samples (n // 256 equal).
All inputs are finite; a program needn't handle non-finite values.
Results may differ from a plain program's by a relative error of at most 0.0003.
Values sent between devices are 32-bit elements; how exact they have to be, the bound alone decides.
A program may use at most 64 MiB of HBM per device.

v0:
```python
import math

import jax
import jax.numpy as jnp
from jax import lax
from jax.sharding import PartitionSpec as P

NB = 2048
NQ = 128
NP = 16
SFT_DEV = 8
MAXD = 1000
NFRAC = 8
RUN = 256


stat_eps = 1e-06
floor_share = 0.5


def shifted(value, axis, by):
    length = lax.axis_size(axis)
    pairs = [(i, i + by) for i in range(length) if 0 <= i + by < length]
    return lax.ppermute(value, axis, pairs)


def lagrange(fraction):
    return (
        -fraction * (fraction - 1.0) * (fraction - 2.0) / 6.0,
        (fraction + 1.0) * (fraction - 1.0) * (fraction - 2.0) / 2.0,
        -(fraction + 1.0) * fraction * (fraction - 2.0) / 2.0,
        (fraction + 1.0) * fraction * (fraction - 1.0) / 6.0,
    )


def phase_pair(product, modulus, direction):
    angles = direction * 2.0 * math.pi / modulus * (product % modulus).astype(jnp.float32)
    return (jnp.cos(angles), jnp.sin(angles))


def dft_table(length, direction):
    rows_at = lax.broadcasted_iota(jnp.int32, (length, length), 0)
    cols_at = lax.broadcasted_iota(jnp.int32, (length, length), 1)
    return phase_pair(rows_at * cols_at, length, direction)


def complex_einsum(pattern, lhs_pair, rhs_pair):
    lhs_real, lhs_imag = lhs_pair
    rhs_real, rhs_imag = rhs_pair
    high = lax.Precision.HIGHEST
    out_real = jnp.einsum(pattern, lhs_real, rhs_real, precision=high) - jnp.einsum(
        pattern, lhs_imag, rhs_imag, precision=high
    )
    out_imag = jnp.einsum(pattern, lhs_real, rhs_imag, precision=high) + jnp.einsum(
        pattern, lhs_imag, rhs_real, precision=high
    )
    return (out_real, out_imag)


def rotate(values, phases):
    val_real, val_imag = values
    cos_part, sin_part = phases
    return (val_real * cos_part - val_imag * sin_part, val_real * sin_part + val_imag * cos_part)


def apply_weights(arrived):
    return arrived[:, 1][:, :, None] * arrived[:, 0][:, None]


def finish(arrived):
    owners = lax.axis_size("tm") * lax.axis_size("band")
    my_rank = lax.axis_index("tm") * lax.axis_size("band") + lax.axis_index("band")
    q_local = arrived.shape[3]
    lane_width = arrived.shape[5]
    sample_total = SFT_DEV * owners * NB
    section_one = complex_einsum(
        "abqix,ic->abqcx", (arrived[:, :, 0], arrived[:, :, 1]), dft_table(owners, -1.0)
    )
    c_pos = lax.broadcasted_iota(jnp.int32, (owners, lane_width), 0)
    x_pos = lax.broadcasted_iota(jnp.int32, (owners, lane_width), 1)
    section_one = rotate(section_one, phase_pair(c_pos * (x_pos // NP), SFT_DEV * owners, -1.0))
    short_table = dft_table(SFT_DEV, -1.0)
    ident_rows = jnp.eye(NP, dtype=jnp.float32)
    spread = (jnp.kron(short_table[0], ident_rows), jnp.kron(short_table[1], ident_rows))
    section_two = complex_einsum("abqcx,xy->abqcy", section_one, spread)
    q_grid = my_rank * q_local + lax.broadcasted_iota(jnp.int32, (q_local, owners, lane_width), 0)
    c_grid = lax.broadcasted_iota(jnp.int32, (q_local, owners, lane_width), 1)
    x_grid = lax.broadcasted_iota(jnp.int32, (q_local, owners, lane_width), 2)
    time_index = x_grid % NP + NP * q_grid
    freq_index = c_grid + owners * (x_grid // NP)
    section_two = rotate(section_two, phase_pair(time_index * freq_index, sample_total, -1.0))
    packed = jnp.stack(section_two, axis=2)
    turned = lax.all_to_all(packed, ("tm", "band"), split_axis=4, concat_axis=3, tiled=True)
    turned = turned.reshape(turned.shape[0], 2, 2, NQ, lane_width)
    section_three = complex_einsum(
        "abqx,qv->abvx", (turned[:, :, 0], turned[:, :, 1]), dft_table(NQ, -1.0)
    )
    v_pos = lax.broadcasted_iota(jnp.int32, (NQ, lane_width), 0)
    p_pos = lax.broadcasted_iota(jnp.int32, (NQ, lane_width), 1) % NP
    section_three = rotate(section_three, phase_pair(v_pos * p_pos, NB, -1.0))
    fine_table = dft_table(NP, -1.0)
    ident_blocks = jnp.eye(SFT_DEV, dtype=jnp.float32)
    block_table = (jnp.kron(ident_blocks, fine_table[0]), jnp.kron(ident_blocks, fine_table[1]))
    result = complex_einsum("abvx,xy->abvy", section_three, block_table)
    return jnp.stack(result, axis=2)


def per_device(sft_bins, delay_code, antenna):
    owners = lax.axis_size("tm") * lax.axis_size("band")
    sample_total = SFT_DEV * owners * NB
    spectra = lax.all_to_all(sft_bins, "band", split_axis=1, concat_axis=2, tiled=True)
    bin_grid = spectra.reshape(2, SFT_DEV, NP, NQ)
    section_one = complex_einsum("pk,skl->spl", dft_table(NP, 1.0), (bin_grid[0], bin_grid[1]))
    p_rows = lax.broadcasted_iota(jnp.int32, (NP, NQ), 0)
    l_cols = lax.broadcasted_iota(jnp.int32, (NP, NQ), 1)
    section_one = rotate(section_one, phase_pair(p_rows * l_cols, NB, 1.0))
    series_pair = complex_einsum("spl,lq->spq", section_one, dft_table(NQ, 1.0))
    norm_scale = 1.0 / math.sqrt(NB)
    stacked = jnp.stack([series_pair[0] * norm_scale, series_pair[1] * norm_scale])
    rim_cols = (MAXD + 1 + NP) // NP
    head_rim = stacked[:, 0, :, :rim_cols]
    tail_rim = stacked[:, SFT_DEV - 1, :, NQ - rim_cols :]
    after_rim = shifted(head_rim, ("tm", "band"), -1)
    before = shifted(tail_rim, ("tm", "band"), 1)
    rim_size = NP * rim_cols
    span_len = SFT_DEV * NB
    timed = stacked.transpose(0, 1, 3, 2).reshape(2, span_len)
    before_timed = before.transpose(0, 2, 1).reshape(2, rim_size)
    after_timed = after_rim.transpose(0, 2, 1).reshape(2, rim_size)
    buffer = jnp.concatenate([before_timed, timed, after_timed], axis=1)
    lane_width = SFT_DEV * NP
    tmpl_local = delay_code.shape[0]
    run_count = span_len // RUN
    code_time = (
        delay_code.reshape(tmpl_local, NQ, SFT_DEV, NP)
        .transpose(0, 2, 1, 3)
        .reshape(tmpl_local, run_count, RUN)
    )
    offsets = code_time[:, :, 0] // NFRAC - MAXD
    run_starts = (jnp.arange(run_count, dtype=jnp.int32) * RUN)[None, :] + offsets + (rim_size - 1)

    def take_segment(start):
        return lax.dynamic_slice_in_dim(buffer, start, RUN + 3, 1)

    segments = jax.vmap(jax.vmap(take_segment))(run_starts)
    fraction = (code_time % NFRAC).astype(jnp.float32) / NFRAC
    coeffs = lagrange(fraction)
    res_time = coeffs[0][:, :, None, :] * segments[:, :, :, 0:RUN]
    for tap_index in range(1, 4):
        res_time = (
            res_time
            + coeffs[tap_index][:, :, None, :] * segments[:, :, :, tap_index : tap_index + RUN]
        )
    resampled = res_time.transpose(0, 2, 1, 3).reshape(tmpl_local, 2, SFT_DEV, NQ, NP)
    resampled = resampled.transpose(0, 1, 3, 2, 4).reshape(tmpl_local, 2, NQ, lane_width)
    weight_a = antenna[:, 0]
    weight_b = antenna[:, 1]
    local_sums = jnp.stack(
        [
            jnp.sum(weight_a * weight_a, axis=(1, 2)),
            jnp.sum(weight_b * weight_b, axis=(1, 2)),
            jnp.sum(weight_a * weight_b, axis=(1, 2)),
        ],
        axis=1,
    )
    totals = lax.psum(local_sums, ("tm", "band"))
    payload = jnp.stack([resampled, antenna], axis=1)
    spectra_out = finish(
        apply_weights(
            lax.all_to_all(
                payload[:, :, :, :, None, :],
                ("tm", "band"),
                split_axis=3,
                concat_axis=4,
                tiled=True,
            )
        )
    )
    out_scale = 1.0 / math.sqrt(sample_total)
    a_real = spectra_out[:, 0, 0] * out_scale
    a_imag = spectra_out[:, 0, 1] * out_scale
    b_real = spectra_out[:, 1, 0] * out_scale
    b_imag = spectra_out[:, 1, 1] * out_scale
    power_a = (totals[:, 0] / sample_total + stat_eps)[:, None, None]
    power_b = (totals[:, 1] / sample_total + stat_eps)[:, None, None]
    cross_ab = (totals[:, 2] / sample_total)[:, None, None]
    det_floor = jnp.maximum(
        power_a * power_b - cross_ab * cross_ab, floor_share * power_a * power_b
    )
    f_stat = (
        power_b * (a_real * a_real + a_imag * a_imag)
        + power_a * (b_real * b_real + b_imag * b_imag)
        - 2.0 * cross_ab * (a_real * b_real + a_imag * b_imag)
    ) / det_floor
    return f_stat[:, :, None, :]


def solution(mesh):
    in_specs = (
        P(None, ("groups", "tm"), "band"),
        P(("groups", "tmpl"), None, ("tm", "band")),
        P(("groups", "tmpl"), None, None, ("tm", "band")),
    )
    out_specs = P(("groups", "tmpl"), None, ("tm", "band"), None)
    return jax.shard_map(
        per_device, mesh=mesh, in_specs=in_specs, out_specs=out_specs, check_vma=False
    )
```

profile of v0, /device:TPU:0, one launch (start us, length us, event | category | flops | bytes accessed | tf_op | source)
XLA Modules:
  0.0 251.3 jit_solution(13160571256986657289)
XLA Ops:
  0.0 1.7 copy.101
  1.7 4.2 %all-to-all-start = ((f32[2,16,1024]{2,0,1:T(2,128)}), f32[2,16,1024]{2,0,1:T(2,128)S(1)}, u32[]{:S(2)}, u32[]{:S(2)}) async-start(f32[2,16,1024]{2,0,1:T(2,128)} %copy.101), calls=%async_computation | async-start | bytes 262144 | tf_op jit(solution)/shard_map/all_to_all | solution.py:111
  6.1 1.8 copy.116
  7.9 1.1 multiply_reduce_fusion.2
  8.9 1.0 copy.99
  14.8 4.0 %collective-permute-start = (f32[2,16,63]{2,1,0:T(8,128)S(1)}, f32[2,16,63]{2,1,0:T(8,128)S(1)}, u32[]{:S(2)}, u32[]{:S(2)}) collective-permute-start(f32[2,16,63]{2,1,0:T(8,128)S(1)} %get-tuple-element.51), channel_id=1, source_target_pairs={{0,2},{2,4},{4,6},{6,8},{8,10},{10,12},{12,14},{1,3},{3,5},{5,7},{... | collective-permute-start | bytes 24200 | tf_op jit(solution)/shard_map/ppermute | solution.py:24
  18.8 1.3 collective-permute-start.1
  21.2 3.2 %collective-permute-done.1 = f32[2,16,63]{2,1,0:T(8,128)S(1)} collective-permute-done((f32[2,16,63]{2,1,0:T(8,128)S(1)}, f32[2,16,63]{2,1,0:T(8,128)S(1)}, u32[]{:S(2)}, u32[]{:S(2)}) %collective-permute-start.1) | collective-permute-done | bytes 8096 | tf_op jit(solution)/shard_map/ppermute | solution.py:24
  24.9 168.8 %while.1 = (s32[]{:T(128)}, f32[2,18400]{1,0:T(2,128)S(1)}, s32[128,2]{1,0:T(8,128)S(1)}, f32[128,2,259]{2,1,0:T(2,128)S(1)}, s32[]{:T(128)}) while((s32[]{:T(128)}, f32[2,18400]{1,0:T(2,128)S(1)}, s32[128,2]{1,0:T(8,128)S(1)}, f32[128,2,259]{2,1,0:T(2,128)S(1)}, s32[]{:T(128)}) %tuple.47), condition=%wide.while_cond, body=%wide.while_body.sunk | while | flops 2 | bytes 6241 | solution.py:143
  26.9 0.7 bitcast_dynamic-update-slice_fusion.2
  30.8 0.7 bitcast_dynamic-update-slice_fusion.2
  33.5 0.7 bitcast_dynamic-update-slice_fusion.2
  34.8 0.7 bitcast_dynamic-update-slice_fusion.2
  37.4 0.7 bitcast_dynamic-update-slice_fusion.2
  41.4 0.7 bitcast_dynamic-update-slice_fusion.2
  45.3 0.7 bitcast_dynamic-update-slice_fusion.2
  48.0 0.7 bitcast_dynamic-update-slice_fusion.2
  51.9 0.7 bitcast_dynamic-update-slice_fusion.2
  55.9 0.7 bitcast_dynamic-update-slice_fusion.2
  58.5 0.7 bitcast_dynamic-update-slice_fusion.2
  59.8 0.7 bitcast_dynamic-update-slice_fusion.2
  62.5 0.7 bitcast_dynamic-update-slice_fusion.2
  66.4 0.7 bitcast_dynamic-update-slice_fusion.2
  70.4 0.7 bitcast_dynamic-update-slice_fusion.2
  73.0 0.7 bitcast_dynamic-update-slice_fusion.2
  77.0 0.7 bitcast_dynamic-update-slice_fusion.2
  80.9 0.7 bitcast_dynamic-update-slice_fusion.2
  83.6 0.7 bitcast_dynamic-update-slice_fusion.2
  84.9 0.7 bitcast_dynamic-update-slice_fusion.2
  87.5 0.7 bitcast_dynamic-update-slice_fusion.2
  91.5 0.7 bitcast_dynamic-update-slice_fusion.2
  95.5 0.7 bitcast_dynamic-update-slice_fusion.2
  98.1 0.7 bitcast_dynamic-update-slice_fusion.2
  102.1 0.7 bitcast_dynamic-update-slice_fusion.2
  106.0 0.7 bitcast_dynamic-update-slice_fusion.2
  108.6 0.7 bitcast_dynamic-update-slice_fusion.2
  110.0 0.7 bitcast_dynamic-update-slice_fusion.2
  112.6 0.7 bitcast_dynamic-update-slice_fusion.2
  116.6 0.7 bitcast_dynamic-update-slice_fusion.2
  120.5 0.7 bitcast_dynamic-update-slice_fusion.2
  123.2 0.7 bitcast_dynamic-update-slice_fusion.2
  127.1 0.7 bitcast_dynamic-update-slice_fusion.2
  131.1 0.7 bitcast_dynamic-update-slice_fusion.2
  133.7 0.7 bitcast_dynamic-update-slice_fusion.2
  135.0 0.7 bitcast_dynamic-update-slice_fusion.2
  137.7 0.7 bitcast_dynamic-update-slice_fusion.2
  141.6 0.7 bitcast_dynamic-update-slice_fusion.2
  145.6 0.7 bitcast_dynamic-update-slice_fusion.2
  148.2 0.7 bitcast_dynamic-update-slice_fusion.2
  152.2 0.7 bitcast_dynamic-update-slice_fusion.2
  156.1 0.7 bitcast_dynamic-update-slice_fusion.2
  158.8 0.7 bitcast_dynamic-update-slice_fusion.2
  160.1 0.7 bitcast_dynamic-update-slice_fusion.2
  162.7 0.7 bitcast_dynamic-update-slice_fusion.2
  166.7 0.7 bitcast_dynamic-update-slice_fusion.2
  193.8 0.9 fusion.214
  196.0 1.0 maximum_bitcast_fusion
  197.0 1.0 copy.117
  198.0 5.8 %all-to-all-start.1 = ((f32[2,2,2,128,1,128]{5,2,0,1,4,3:T(2,128)}), f32[2,2,2,128,1,128]{5,2,0,1,4,3:T(2,128)S(1)}, u32[]{:S(2)}, u32[]{:S(2)}) async-start(f32[2,2,2,128,1,128]{5,2,0,1,4,3:T(2,128)} %copy.117), calls=%async_computation.1 | async-start | bytes 1048576 | tf_op jit(solution)/shard_map/all_to_all | solution.py:170
  203.8 22.1 %psum.7 = f32[2,3]{0,1:T(4,128)S(1)} all-reduce(f32[2,3]{0,1:T(4,128)S(1)} %pad_maximum_fusion.2), channel_id=1, replica_groups=mesh['groups'=2,'tm'=4,'band'=2,'tmpl'=2] {'tm','band'}, use_global_device_ids=true, to_apply=%region_3.4 | all-reduce | flops 6 | bytes 48 | tf_op jit(solution)/shard_map/psum | solution.py:166
  230.8 0.9 copy.123
  231.7 3.7 %all-to-all-start.2 = ((f32[2,2,2,16,8,128]{5,3,1,0,2,4:T(8,128)}), f32[2,2,2,16,8,128]{5,3,1,0,2,4:T(8,128)S(1)}, u32[]{:S(2)}, u32[]{:S(2)}) async-start(f32[2,2,2,16,8,128]{5,3,1,0,2,4:T(8,128)} %copy.123), calls=%async_computation.2 | async-start | bytes 1048576 | tf_op jit(solution)/shard_map/all_to_all | solution.py:93
  236.0 10.3 %all-to-all-done.2 = f32[2,2,2,16,8,128]{5,3,1,0,2,4:T(8,128)S(1)} async-done(((f32[2,2,2,16,8,128]{5,3,1,0,2,4:T(8,128)}), f32[2,2,2,16,8,128]{5,3,1,0,2,4:T(8,128)S(1)}, u32[]{:S(2)}, u32[]{:S(2)}) %all-to-all-start.2) | async-done | bytes 524320 | tf_op jit(solution)/shard_map/all_to_all | solution.py:93
  250.5 0.8 fusion.36
  (421 shorter events, 152.5 us)
Async XLA Ops:
  1.7 9.7 %all-to-all-start = ((f32[2,16,1024]{2,0,1:T(2,128)}), f32[2,16,1024]{2,0,1:T(2,128)S(1)}, u32[]{:S(2)}, u32[]{:S(2)}) async-start(f32[2,16,1024]{2,0,1:T(2,128)} %copy.101), calls=%async_computation | async-start | bytes 262144 | tf_op jit(solution)/shard_map/all_to_all | solution.py:111
  14.8 6.3 %collective-permute-start = (f32[2,16,63]{2,1,0:T(8,128)S(1)}, f32[2,16,63]{2,1,0:T(8,128)S(1)}, u32[]{:S(2)}, u32[]{:S(2)}) collective-permute-start(f32[2,16,63]{2,1,0:T(8,128)S(1)} %get-tuple-element.51), channel_id=1, source_target_pairs={{0,2},{2,4},{4,6},{6,8},{8,10},{10,12},{12,14},{1,3},{3,5},{5,7},{... | collective-permute-start | bytes 24200 | tf_op jit(solution)/shard_map/ppermute | solution.py:24
  18.8 5.6 %collective-permute-start.1 = (f32[2,16,63]{2,1,0:T(8,128)S(1)}, f32[2,16,63]{2,1,0:T(8,128)S(1)}, u32[]{:S(2)}, u32[]{:S(2)}) collective-permute-start(f32[2,16,63]{2,1,0:T(8,128)S(1)} %get-tuple-element.50), channel_id=1, source_target_pairs={{2,0},{4,2},{6,4},{8,6},{10,8},{12,10},{14,12},{3,1},{5,3},{7,5},{... | collective-permute-start | bytes 24200 | tf_op jit(solution)/shard_map/ppermute | solution.py:24
  198.0 29.2 %all-to-all-start.1 = ((f32[2,2,2,128,1,128]{5,2,0,1,4,3:T(2,128)}), f32[2,2,2,128,1,128]{5,2,0,1,4,3:T(2,128)S(1)}, u32[]{:S(2)}, u32[]{:S(2)}) async-start(f32[2,2,2,128,1,128]{5,2,0,1,4,3:T(2,128)} %copy.117), calls=%async_computation.1 | async-start | bytes 1048576 | tf_op jit(solution)/shard_map/all_to_all | solution.py:170
  231.7 14.6 %all-to-all-start.2 = ((f32[2,2,2,16,8,128]{5,3,1,0,2,4:T(8,128)}), f32[2,2,2,16,8,128]{5,3,1,0,2,4:T(8,128)S(1)}, u32[]{:S(2)}, u32[]{:S(2)}) async-start(f32[2,2,2,16,8,128]{5,3,1,0,2,4:T(8,128)} %copy.123), calls=%async_computation.2 | async-start | bytes 1048576 | tf_op jit(solution)/shard_map/all_to_all | solution.py:93
where the time goes:
time: 253 us; the launch traced here: 251 us
  local copies, waits for them, and re-layouts  181 us (72%)
  blocking collectives  22.1 us (9%)
  starting transfers between devices  18.9 us (7%)
  waiting for transfers between devices  13.5 us (5%)
  matrix products  10.2 us (4%)
  other arithmetic  4.66 us (2%)
    gather x384, local copies, waits for them, and re-layouts  169 us
    psum x1, blocking collectives, per_device(): totals = lax.psum(local_sums, ('tm', 'band'))  22.1 us
    all_to_all x1, waiting for transfers between devices, finish(): lax.all_to_all(packed, ('tm', 'band'), split_axis=4, concat_axis=3, tiled...  10.3 us
    all_to_all x1, starting transfers between devices, per_device(): lax.all_to_all(payload[:, :, :, :, None, :], ('tm', 'band'), split_axis=3...  5.76 us
    ppermute x2, starting transfers between devices, shifted(): return lax.ppermute(value, axis, pairs)  5.31 us
  transfers between devices with their start and end apart: 5, of which 2 were waited for; matrix products, arithmetic and copies ran while one was open for 3% of the time, Pallas kernels for 0%

commit v1 on v0

v1 whole, which is shorter than its diff:
```python
import functools
import math

import jax
import jax.numpy as jnp
import ml_dtypes
import numpy as np
from jax import lax
from jax.experimental import pallas as pl
from jax.experimental.pallas import tpu as pltpu
from jax.sharding import PartitionSpec as P

NB = 2048
NQ = 128
NP = 16
SFT_DEV = 8
MAXD = 1000
NFRAC = 8
RUN = 256
LANES = 128

stat_eps = 1e-06
floor_share = 0.5
MESH = pl.DeviceIdType.MESH


def shifted(value, axis, by):
    length = lax.axis_size(axis)
    pairs = [(i, i + by) for i in range(length) if 0 <= i + by < length]
    return lax.ppermute(value, axis, pairs)


def lagrange(fraction):
    return (
        -fraction * (fraction - 1.0) * (fraction - 2.0) / 6.0,
        (fraction + 1.0) * (fraction - 1.0) * (fraction - 2.0) / 2.0,
        -(fraction + 1.0) * fraction * (fraction - 2.0) / 2.0,
        (fraction + 1.0) * fraction * (fraction - 1.0) / 6.0,
    )


def phase_pair(product, modulus, direction):
    angles = direction * 2.0 * math.pi / modulus * (product % modulus).astype(jnp.float32)
    return (jnp.cos(angles), jnp.sin(angles))


def dft_table(length, direction):
    rows_at = lax.broadcasted_iota(jnp.int32, (length, length), 0)
    cols_at = lax.broadcasted_iota(jnp.int32, (length, length), 1)
    return phase_pair(rows_at * cols_at, length, direction)


def complex_einsum(pattern, lhs_pair, rhs_pair):
    lhs_real, lhs_imag = lhs_pair
    rhs_real, rhs_imag = rhs_pair
    high = lax.Precision.HIGHEST
    out_real = jnp.einsum(pattern, lhs_real, rhs_real, precision=high) - jnp.einsum(
        pattern, lhs_imag, rhs_imag, precision=high
    )
    out_imag = jnp.einsum(pattern, lhs_real, rhs_imag, precision=high) + jnp.einsum(
        pattern, lhs_imag, rhs_real, precision=high
    )
    return (out_real, out_imag)


def rotate(values, phases):
    val_real, val_imag = values
    cos_part, sin_part = phases
    return (val_real * cos_part - val_imag * sin_part, val_real * sin_part + val_imag * cos_part)


def split2(value):
    high = value.astype(jnp.bfloat16)
    return high, (value - high.astype(jnp.float32)).astype(jnp.bfloat16)


def dot3(lhs, rhs):
    lhs_hi, lhs_lo = lhs
    rhs_hi, rhs_lo = rhs
    dot = functools.partial(jnp.dot, preferred_element_type=jnp.float32)
    return dot(lhs_hi, rhs_hi) + (dot(lhs_hi, rhs_lo) + dot(lhs_lo, rhs_hi))


def swap_blocks(blocks):
    count = len(blocks)
    width = LANES // count
    blocks = list(blocks)
    lane_block = lax.broadcasted_iota(jnp.int32, blocks[0].shape, 1) // width
    half = count // 2
    while half:
        keep = (lane_block & half) == 0
        for i in range(count):
            if i & half == 0:
                low, high = blocks[i], blocks[i + half]
                blocks[i] = jnp.where(keep, low, pltpu.roll(high, half * width, 1))
                blocks[i + half] = jnp.where(
                    keep, pltpu.roll(low, LANES - half * width, 1), high
                )
        half //= 2
    return blocks


def grid_to_time(ref, index, out_ref, out_index):
    rows = ref.shape[-2]
    per = rows // SFT_DEV
    blocks = [ref[index + (pl.ds(i, per, stride=SFT_DEV),)] for i in range(SFT_DEV)]
    for j, block in enumerate(swap_blocks(blocks)):
        out_ref[out_index + (slice(j * per, (j + 1) * per),)] = block


def resample_kernel(start_ref, buf_ref, code_ref, ant_ref, x_ref, sums_ref, code_t, ant_t, seg):
    tmpl_local = code_ref.shape[0]
    rows = code_ref.shape[1]
    runs = start_ref.shape[1]
    lane = lax.broadcasted_iota(jnp.int32, (8, LANES), 1)
    wide_lane = lax.broadcasted_iota(jnp.int32, (runs, LANES), 1)
    sums_ref[...] = jnp.zeros_like(sums_ref)
    for t in range(tmpl_local):
        for r in range(runs):
            start = start_ref[t, r]
            row = start // LANES
            shift = start % LANES
            held = buf_ref[pl.ds(2 * row, 8), :]
            turned = pltpu.roll(held, LANES - shift, 1)
            below = pltpu.roll(turned, 6, 0)
            seg[8 * r : 8 * r + 8, :] = jnp.where(lane < LANES - shift, turned, below)
        grid_to_time(code_ref, (t,), code_t, ())
        for w in range(2):
            grid_to_time(ant_ref, (t, w), ant_t, (w,))
        wa = ant_t[0]
        wb = ant_t[1]
        for k, product in enumerate((wa * wa, wb * wb, wa * wb)):
            sums_ref[3 * t + k : 3 * t + k + 1, :] = jnp.sum(product, axis=0, keepdims=True)
        taps = []
        for c in range(2):
            lines = [seg[pl.ds(2 * r + c, runs, stride=8), :] for r in range(3)]
            moved = [lines] + [
                [pltpu.roll(line, LANES - k, 1) for line in lines] for k in range(1, 4)
            ]
            taps.append(moved)
        for r in range(2):
            code = code_t[pl.ds(r, runs, stride=2), :]
            fraction = (code & (NFRAC - 1)).astype(jnp.float32) * (1.0 / NFRAC)
            coeffs = lagrange(fraction)
            wts = [ant_t[w, pl.ds(r, runs, stride=2), :] for w in range(2)]
            for c in range(2):
                moved = taps[c]
                total = coeffs[0] * moved[0][r]
                for k in range(1, 4):
                    total = total + coeffs[k] * jnp.where(
                        wide_lane < LANES - k, moved[k][r], moved[k][r + 1]
                    )
                for w in range(2):
                    x_ref[2 * t + w, c, pl.ds(r, runs, stride=2), :] = total * wts[w]


def bit_reverse(index, bits):
    out = 0
    for k in range(bits):
        out = out + ((index // (1 << k)) % 2) * (1 << (bits - 1 - k))
    return out


def spectrum_kernel(
    band_size,
    bits,
    sample_total,
    fact_ref,
    x_ref,
    sums_ref,
    left_ref,
    twid_ref,
    right_hi_ref,
    right_lo_ref,
    out_ref,
    cur,
    got,
    cur_sums,
    got_sums,
    stat,
    stat_got,
    send_sem,
    recv_sem,
    last_send,
    last_recv,
):
    chunks = x_ref.shape[0]
    tmpl_local = chunks // 2
    me = lax.axis_index("tm") * band_size + lax.axis_index("band")

    def place(rank):
        return {"tm": rank // band_size, "band": rank % band_size}

    home = bit_reverse(me, bits)
    partners = []
    for st in range(bits):
        half = 1 << (bits - 1 - st)
        partners.append(me + half - 2 * half * ((me // half) % 2))
    barrier = pltpu.get_barrier_semaphore()
    for partner in partners:
        pl.semaphore_signal(barrier, inc=1, device_id=place(partner), device_id_type=MESH)

    @pl.when(home != me)
    def _():
        pl.semaphore_signal(barrier, inc=1, device_id=place(home), device_id_type=MESH)
        pl.semaphore_wait(barrier, bits + 1)

    @pl.when(home == me)
    def _():
        pl.semaphore_wait(barrier, bits)

    def data_copy(st, ch):
        return pltpu.make_async_remote_copy(
            src_ref=x_ref.at[ch] if st == 0 else cur.at[st - 1, ch],
            dst_ref=got.at[st, ch],
            send_sem=send_sem.at[st, ch],
            recv_sem=recv_sem.at[st, ch],
            device_id=place(partners[st]),
            device_id_type=MESH,
        )

    def sums_copy(st):
        return pltpu.make_async_remote_copy(
            src_ref=sums_ref if st == 0 else cur_sums.at[st - 1],
            dst_ref=got_sums.at[st],
            send_sem=send_sem.at[st, chunks],
            recv_sem=recv_sem.at[st, chunks],
            device_id=place(partners[st]),
            device_id_type=MESH,
        )

    copies = {}
    for ch in range(chunks):
        copies[0, ch] = data_copy(0, ch)
        copies[0, ch].start()
    sums_copies = [sums_copy(0)]
    sums_copies[0].start()
    left = split2(left_ref[...])
    spectra = {}
    norm = 1.0 / math.sqrt(sample_total)

    def transform(ch):
        value = cur[bits - 1, ch].reshape(2 * NQ, LANES)
        mixed = dot3(left, split2(value))
        real, imag = mixed[:NQ], mixed[NQ:]
        cos_part, sin_part = twid_ref[0], twid_ref[1]
        line = jnp.concatenate(
            [real * cos_part - imag * sin_part, real * sin_part + imag * cos_part], axis=1
        )
        out = dot3(split2(line), (right_hi_ref[...], right_lo_ref[...])) * norm
        spectra[ch] = (out[:, :LANES], out[:, LANES:])

    totals = []
    last = []

    def last_copy(t):
        return pltpu.make_async_remote_copy(
            src_ref=stat.at[t],
            dst_ref=stat_got.at[t],
            send_sem=last_send.at[t],
            recv_sem=last_recv.at[t],
            device_id=place(home),
            device_id_type=MESH,
        )

    def statistic(t):
        if not totals:
            for st in range(bits):
                sums_copies[st].wait()
                before = sums_ref[...] if st == 0 else cur_sums[st - 1]
                cur_sums[st] = before + got_sums[st]
                if st + 1 < bits:
                    sums_copies.append(sums_copy(st + 1))
                    sums_copies[st + 1].start()
            totals.append(jnp.sum(cur_sums[bits - 1], axis=1, keepdims=True) / sample_total)
        total = totals[0]
        power_a = total[3 * t : 3 * t + 1] + stat_eps
        power_b = total[3 * t + 1 : 3 * t + 2] + stat_eps
        cross_ab = total[3 * t + 2 : 3 * t + 3]
        det = jnp.maximum(
            power_a * power_b - cross_ab * cross_ab, floor_share * power_a * power_b
        )
        (a_real, a_imag), (b_real, b_imag) = spectra[2 * t], spectra[2 * t + 1]
        value = (
            power_b * (a_real * a_real + a_imag * a_imag)
            + power_a * (b_real * b_real + b_imag * b_imag)
            - 2.0 * cross_ab * (a_real * b_real + a_imag * b_imag)
        ) / det
        per = NQ // SFT_DEV
        blocks = swap_blocks([value[i * per : (i + 1) * per] for i in range(SFT_DEV)])
        for j, block in enumerate(blocks):
            stat[t, j * per : (j + 1) * per, :] = block

        @pl.when(home != me)
        def _():
            last_copy(t).start()

        @pl.when(home == me)
        def _():
            out_ref[t] = stat[t]

    order = sorted(
        ((st, ch) for st in range(bits) for ch in range(chunks)), key=lambda p: (p[0] + p[1], p[0])
    )
    for st, ch in order:
        copies[st, ch].wait_recv()
        own = x_ref[ch] if st == 0 else cur[st - 1, ch]
        other = got[st, ch]
        base = (me * bits + st) * 3
        sign, w_real, w_imag = (fact_ref[base + k] for k in range(3))
        mixed = sign * own + other
        cur[st, ch, 0] = mixed[0] * w_real - mixed[1] * w_imag
        cur[st, ch, 1] = mixed[0] * w_imag + mixed[1] * w_real
        if st + 1 < bits:
            copies[st + 1, ch] = data_copy(st + 1, ch)
            copies[st + 1, ch].start()
        else:
            transform(ch)
            if ch % 2:
                statistic(ch // 2)

    for t in range(tmpl_local):

        @pl.when(home != me)
        def _():
            last_copy(t).wait()
            out_ref[t] = stat_got[t]

    for copy in copies.values():
        copy.wait_send()


def butterfly_factors(owners, bits):
    table = np.zeros((owners, bits, 3), np.float32)
    for i in range(owners):
        for st in range(bits):
            half = owners >> (st + 1)
            upper = (i // half) % 2
            angle = -2.0 * math.pi * (i % half) / (2 * half) if upper else 0.0
            table[i, st] = (-1.0 if upper else 1.0, math.cos(angle), math.sin(angle))
    return table.reshape(-1)


def per_device(sft_bins, delay_code, antenna):
    band_size = lax.axis_size("band")
    owners = lax.axis_size("tm") * band_size
    bits = owners.bit_length() - 1
    sample_total = SFT_DEV * owners * NB
    me = lax.axis_index("tm") * band_size + lax.axis_index("band")
    spectra = lax.all_to_all(sft_bins, "band", split_axis=1, concat_axis=2, tiled=True)
    bin_grid = spectra.reshape(2, SFT_DEV, NP, NQ)
    section_one = complex_einsum("pk,skl->spl", dft_table(NP, 1.0), (bin_grid[0], bin_grid[1]))
    p_rows = lax.broadcasted_iota(jnp.int32, (NP, NQ), 0)
    l_cols = lax.broadcasted_iota(jnp.int32, (NP, NQ), 1)
    section_one = rotate(section_one, phase_pair(p_rows * l_cols, NB, 1.0))
    series_pair = complex_einsum("spl,lq->spq", section_one, dft_table(NQ, 1.0))
    norm_scale = 1.0 / math.sqrt(NB)
    stacked = jnp.stack([series_pair[0] * norm_scale, series_pair[1] * norm_scale])
    rim_cols = 72
    head_rim = stacked[:, 0, :, :rim_cols]
    tail_rim = stacked[:, SFT_DEV - 1, :, NQ - rim_cols :]
    after_rim = shifted(head_rim, ("tm", "band"), -1)
    before = shifted(tail_rim, ("tm", "band"), 1)
    rim_size = NP * rim_cols
    span_len = SFT_DEV * NB
    timed = stacked.transpose(0, 1, 3, 2).reshape(2, span_len)
    before_timed = before.transpose(0, 2, 1).reshape(2, rim_size)
    after_timed = after_rim.transpose(0, 2, 1).reshape(2, rim_size)
    buffer = jnp.concatenate([before_timed, timed, after_timed], axis=1)
    buffer = buffer.reshape(2, -1, LANES).transpose(1, 0, 2).reshape(-1, LANES)
    tmpl_local = delay_code.shape[0]
    run_count = span_len // RUN
    run_cols = RUN // NP
    offsets = delay_code[:, ::run_cols, ::NP].transpose(0, 2, 1).reshape(tmpl_local, run_count)
    offsets = offsets // NFRAC - MAXD
    starts = (jnp.arange(run_count, dtype=jnp.int32) * RUN)[None, :] + offsets + (rim_size - 1)

    vmem = pl.BlockSpec(memory_space=pltpu.VMEM)
    smem = pl.BlockSpec(memory_space=pltpu.SMEM)
    planes = (2 * tmpl_local, 2, NQ, LANES)
    x, sums = pl.pallas_call(
        resample_kernel,
        out_shape=(
            jax.ShapeDtypeStruct(planes, jnp.float32),
            jax.ShapeDtypeStruct((8, LANES), jnp.float32),
        ),
        in_specs=[smem, vmem, vmem, vmem],
        out_specs=(vmem, vmem),
        scratch_shapes=[
            pltpu.VMEM((NQ, LANES), jnp.int32),
            pltpu.VMEM((2, NQ, LANES), jnp.float32),
            pltpu.VMEM((8 * run_count, LANES), jnp.float32),
        ],
        compiler_params=pltpu.CompilerParams(vmem_limit_bytes=32 * 1024 * 1024),
    )(starts, buffer, delay_code, antenna)

    home = bit_reverse(me, bits)
    per = NQ // SFT_DEV
    row_at = lax.broadcasted_iota(jnp.int32, (NQ, LANES), 0)
    col_at = lax.broadcasted_iota(jnp.int32, (NQ, LANES), 1)
    coarse = (row_at // per + SFT_DEV * (row_at % per)) * owners + home
    cos_left, sin_left = phase_pair(coarse * col_at, NQ * owners, -1.0)
    left = jnp.concatenate(
        [
            jnp.concatenate([cos_left, -sin_left], axis=1),
            jnp.concatenate([sin_left, cos_left], axis=1),
        ],
        axis=0,
    )
    twid = jnp.stack(phase_pair(coarse * col_at, sample_total, -1.0))
    col = np.arange(LANES)
    fine = col // NP + SFT_DEV * (col % NP)
    angles = -2.0 * np.pi / LANES * ((np.arange(LANES)[:, None] * fine[None, :]) % LANES)
    right = np.block([[np.cos(angles), np.sin(angles)], [-np.sin(angles), np.cos(angles)]])
    right_hi = right.astype(ml_dtypes.bfloat16)
    right_lo = (right - right_hi.astype(np.float64)).astype(ml_dtypes.bfloat16)
    out = pl.pallas_call(
        functools.partial(spectrum_kernel, band_size, bits, sample_total),
        out_shape=jax.ShapeDtypeStruct((tmpl_local, NQ, LANES), jnp.float32),
        in_specs=[smem] + [vmem] * 6,
        out_specs=vmem,
        scratch_shapes=[
            pltpu.VMEM((bits,) + planes, jnp.float32),
            pltpu.VMEM((bits,) + planes, jnp.float32),
            pltpu.VMEM((bits, 8, LANES), jnp.float32),
            pltpu.VMEM((bits, 8, LANES), jnp.float32),
            pltpu.VMEM((tmpl_local, NQ, LANES), jnp.float32),
            pltpu.VMEM((tmpl_local, NQ, LANES), jnp.float32),
            pltpu.SemaphoreType.DMA((bits, planes[0] + 1)),
            pltpu.SemaphoreType.DMA((bits, planes[0] + 1)),
            pltpu.SemaphoreType.DMA((tmpl_local,)),
            pltpu.SemaphoreType.DMA((tmpl_local,)),
        ],
        compiler_params=pltpu.CompilerParams(
            collective_id=0, has_side_effects=True, vmem_limit_bytes=40 * 1024 * 1024
        ),
    )(
        jnp.asarray(butterfly_factors(owners, bits)),
        x,
        sums,
        left,
        twid,
        jnp.asarray(right_hi),
        jnp.asarray(right_lo),
    )
    return out[:, :, None, :]


def solution(mesh):
    in_specs = (
        P(None, ("groups", "tm"), "band"),
        P(("groups", "tmpl"), None, ("tm", "band")),
        P(("groups", "tmpl"), None, None, ("tm", "band")),
    )
    out_specs = P(("groups", "tmpl"), None, ("tm", "band"), None)
    return jax.shard_map(
        per_device, mesh=mesh, in_specs=in_specs, out_specs=out_specs, check_vma=False
    )
```

time: 253 us -> 74.6 us (0.29)
  the two profiles are of different devices: /device:TPU:0 before, /device:TPU:2 now
where the time goes in v1:
time: 74.6 us; the launch traced here: 74.3 us
  Pallas kernels  51.4 us (69%)
  starting transfers between devices  10.8 us (14%)
  local copies, waits for them, and re-layouts  5.83 us (8%)
  matrix products  2.83 us (4%)
  waiting for transfers between devices  1.98 us (3%)
  other arithmetic  1.08 us (1%)
    pallas_call x1, Pallas kernels, per_device(): pl.pallas_call(functools.partial(spectrum_kernel, band_size, bits, sample...  48.7 us
    ppermute x2, starting transfers between devices, shifted(): return lax.ppermute(value, axis, pairs)  7.47 us
    unnamed x12, local copies, waits for them, and re-layouts  3.79 us
    all_to_all x1, starting transfers between devices, per_device(): lax.all_to_all(sft_bins, 'band', split_axis=1, concat_axis=2, tiled=True)  3.37 us
    pallas_call x1, Pallas kernels, per_device(): pl.pallas_call(resample_kernel, out_shape=(jax.ShapeDtypeStruct(planes, j...  2.72 us
  transfers between devices with their start and end apart: 3, of which 2 were waited for; matrix products, arithmetic and copies ran while one was open for 3% of the time, Pallas kernels for 0%

profile of v1, /device:TPU:2, one launch (start us, length us, event | category | flops | bytes accessed | tf_op | source)
XLA Modules:
  0.0 74.3 jit_solution(281648796233207628)
XLA Ops:
  0.0 1.7 %copy.25 = f32[2,16,1024]{2,0,1:T(2,128)} copy(f32[2,16,1024]{2,1,0:T(8,128)} %param.6) | data formatting | bytes 262144 | tf_op args[0]
  1.7 3.4 %all-to-all-start = ((f32[2,16,1024]{2,0,1:T(2,128)}), f32[2,16,1024]{2,0,1:T(2,128)S(1)}, u32[]{:S(2)}, u32[]{:S(2)}) async-start(f32[2,16,1024]{2,0,1:T(2,128)} %copy.25), calls=%async_computation | async-start | bytes 262144 | tf_op jit(solution)/shard_map/all_to_all | solution.py:350
  5.2 0.0 copy-start.1
  5.2 0.4 fusion.67
  5.6 0.4 fusion.34
  6.0 0.1 copy-done.1
  6.1 0.1 slice.17
  6.2 0.1 copy.24
  6.2 0.1 reshape.333
  6.4 0.1 fusion.59
  6.5 0.9 %all-to-all-done = f32[2,16,1024]{2,0,1:T(2,128)S(1)} async-done(((f32[2,16,1024]{2,0,1:T(2,128)}), f32[2,16,1024]{2,0,1:T(2,128)S(1)}, u32[]{:S(2)}, u32[]{:S(2)}) %all-to-all-start) | async-done | bytes 131104 | tf_op jit(solution)/shard_map/all_to_all | solution.py:350
  7.4 0.1 copy.33
  7.5 0.1 squeeze.13
  7.6 0.2 fusion.49
  7.8 0.1 squeeze.12
  7.9 0.2 fusion.51
  8.2 0.2 convolution_add_fusion.1
  8.4 0.3 convolution_subtract_fusion.1
  8.7 0.5 fusion.20
  9.1 0.5 fusion.14
  9.6 0.5 fusion.3
  10.1 0.5 fusion.1
  10.5 0.1 fusion.38
  10.6 4.0 %collective-permute-start.1 = (f32[2,16,72]{2,1,0:T(8,128)S(1)}, f32[2,16,72]{2,1,0:T(8,128)S(1)}, u32[]{:S(2)}, u32[]{:S(2)}) collective-permute-start(f32[2,16,72]{2,1,0:T(8,128)S(1)} %get-tuple-element.10), channel_id=1, source_target_pairs={{2,0},{4,2},{6,4},{8,6},{10,8},{12,10},{14,12},{3,1},{5,3},{7,5},{... | collective-permute-start | bytes 27656 | tf_op jit(solution)/shard_map/ppermute | solution.py:30
  14.6 3.5 %collective-permute-start = (f32[2,16,72]{2,1,0:T(8,128)S(1)}, f32[2,16,72]{2,1,0:T(8,128)S(1)}, u32[]{:S(2)}, u32[]{:S(2)}) collective-permute-start(f32[2,16,72]{2,1,0:T(8,128)S(1)} %get-tuple-element.9), channel_id=1, source_target_pairs={{0,2},{2,4},{4,6},{6,8},{8,10},{10,12},{12,14},{1,3},{3,5},{5,7},{... | collective-permute-start | bytes 27656 | tf_op jit(solution)/shard_map/ppermute | solution.py:30
  18.1 0.3 copy.28
  18.5 0.6 reshape.335
  19.0 0.0 collective-permute-done.1
  19.0 0.1 copy.29
  19.1 0.1 reshape.336
  19.2 1.0 %collective-permute-done = f32[2,16,72]{2,1,0:T(8,128)S(1)} collective-permute-done((f32[2,16,72]{2,1,0:T(8,128)S(1)}, f32[2,16,72]{2,1,0:T(8,128)S(1)}, u32[]{:S(2)}, u32[]{:S(2)}) %collective-permute-start) | collective-permute-done | bytes 9248 | tf_op jit(solution)/shard_map/ppermute | solution.py:30
  20.3 0.1 copy.27
  20.4 0.1 reshape.334
  20.5 0.1 pad_maximum_fusion.1
  20.5 0.1 reshape.337
  20.7 0.0 copy-start
  20.7 0.1 copy.30
  20.8 0.1 reshape.338.buf_ref
  20.9 0.7 copy-done
  21.6 0.0 copy-start.2
  21.6 0.0 copy-start.3
  21.6 2.7 %shard_map.64 = (f32[4,2,128,128]{3,2,1,0:T(8,128)S(1)}, f32[8,128]{1,0:T(8,128)S(1)}) custom-call(s32[2,64]{1,0:T(2,128)S(1)} %add_add_fusion.start_ref, f32[292,128]{1,0:T(8,128)S(1)} %reshape.338.buf_ref, s32[2,128,128]{2,1,0:T(8,128)S(1)} %copy-done.1, f32[2,2,128,128]{3,2,1,0:T(8,128)S(1)} %copy-done), custom_call_target="tpu_custom_call" | custom-call | tf_op jit(solution)/shard_map/pallas_call | solution.py:381
  24.3 0.0 copy-start.4
  24.4 0.0 copy-done.2
  24.4 0.0 copy-done.3
  24.4 0.6 copy-done.4
  25.0 48.7 %shard_map.65 = f32[2,128,128]{2,1,0:T(8,128)S(1)} custom-call(f32[72]{0:T(128)S(1)} %copy-done.4, f32[4,2,128,128]{3,2,1,0:T(8,128)S(1)} %get-tuple-element.7.x_ref, f32[8,128]{1,0:T(8,128)S(1)} %get-tuple-element.8.sums_ref, f32[256,256]{1,0:T(8,128)S(1)} %maximum_maximum_fusion.left_ref, f32[2,128,128]{2,1,0:T(8,128)S(1)} %pad_maximum_fusion.2.twid_ref, ...), custom_call_target="tpu_custom_call" | custom-call | tf_op jit(solution)/shard_map/pallas_call | solution.py:417
  73.7 0.7 copy.35
  (9 shorter events, 0.1 us)
Async XLA Ops:
  1.7 5.7 %all-to-all-start = ((f32[2,16,1024]{2,0,1:T(2,128)}), f32[2,16,1024]{2,0,1:T(2,128)S(1)}, u32[]{:S(2)}, u32[]{:S(2)}) async-start(f32[2,16,1024]{2,0,1:T(2,128)} %copy.25), calls=%async_computation | async-start | bytes 262144 | tf_op jit(solution)/shard_map/all_to_all | solution.py:350
  5.2 0.9 %copy-start.1 = (s32[2,128,128]{2,1,0:T(8,128)S(1)}, s32[2,128,128]{2,1,0:T(8,128)}, u32[]{:S(2)}) copy-start(s32[2,128,128]{2,1,0:T(8,128)} %code_ref.1) | copy-start | bytes 393220
  10.6 8.4 %collective-permute-start.1 = (f32[2,16,72]{2,1,0:T(8,128)S(1)}, f32[2,16,72]{2,1,0:T(8,128)S(1)}, u32[]{:S(2)}, u32[]{:S(2)}) collective-permute-start(f32[2,16,72]{2,1,0:T(8,128)S(1)} %get-tuple-element.10), channel_id=1, source_target_pairs={{2,0},{4,2},{6,4},{8,6},{10,8},{12,10},{14,12},{3,1},{5,3},{7,5},{... | collective-permute-start | bytes 27656 | tf_op jit(solution)/shard_map/ppermute | solution.py:30
  14.6 5.6 %collective-permute-start = (f32[2,16,72]{2,1,0:T(8,128)S(1)}, f32[2,16,72]{2,1,0:T(8,128)S(1)}, u32[]{:S(2)}, u32[]{:S(2)}) collective-permute-start(f32[2,16,72]{2,1,0:T(8,128)S(1)} %get-tuple-element.9), channel_id=1, source_target_pairs={{0,2},{2,4},{4,6},{6,8},{8,10},{10,12},{12,14},{1,3},{3,5},{5,7},{... | collective-permute-start | bytes 27656 | tf_op jit(solution)/shard_map/ppermute | solution.py:30
  20.7 1.0 %copy-start = (f32[2,2,128,128]{3,2,1,0:T(8,128)S(1)}, f32[2,2,128,128]{3,2,1,0:T(8,128)}, u32[]{:S(2)}) copy-start(f32[2,2,128,128]{3,2,1,0:T(8,128)} %ant_ref.1) | copy-start | bytes 786436
  21.6 2.7 %copy-start.2 = (bf16[256,256]{1,0:T(8,128)(2,1)S(1)}, bf16[256,256]{1,0:T(8,128)(2,1)}, u32[]{:S(2)}) copy-start(bf16[256,256]{1,0:T(8,128)(2,1)} %constant.183.clone.right_hi_ref) | copy-start | bytes 393220
  21.6 2.8 %copy-start.3 = (bf16[256,256]{1,0:T(8,128)(2,1)S(1)}, bf16[256,256]{1,0:T(8,128)(2,1)}, u32[]{:S(2)}) copy-start(bf16[256,256]{1,0:T(8,128)(2,1)} %constant.184.clone.right_lo_ref) | copy-start | bytes 393220
  24.3 0.7 copy-start.4

commit v2 on v0

v2 whole, which is shorter than its diff:
```python
import functools
import math

import jax
import jax.numpy as jnp
import ml_dtypes
import numpy as np
from jax import lax
from jax.experimental import pallas as pl
from jax.experimental.pallas import tpu as pltpu
from jax.sharding import PartitionSpec as P

NB = 2048
NQ = 128
NP = 16
SFT_DEV = 8
MAXD = 1000
NFRAC = 8
RUN = 256
LANES = 128

stat_eps = 1e-06
floor_share = 0.5
MESH = pl.DeviceIdType.MESH


def lagrange(fraction):
    return (
        -fraction * (fraction - 1.0) * (fraction - 2.0) / 6.0,
        (fraction + 1.0) * (fraction - 1.0) * (fraction - 2.0) / 2.0,
        -(fraction + 1.0) * fraction * (fraction - 2.0) / 2.0,
        (fraction + 1.0) * fraction * (fraction - 1.0) / 6.0,
    )


def phase_pair(product, modulus, direction):
    angles = direction * 2.0 * math.pi / modulus * (product % modulus).astype(jnp.float32)
    return (jnp.cos(angles), jnp.sin(angles))


def split2(value):
    high = value.astype(jnp.bfloat16)
    return high, (value - high.astype(jnp.float32)).astype(jnp.bfloat16)


def dot3(lhs, rhs):
    lhs_hi, lhs_lo = lhs
    rhs_hi, rhs_lo = rhs
    dot = functools.partial(jnp.dot, preferred_element_type=jnp.float32)
    return dot(lhs_hi, rhs_hi) + (dot(lhs_hi, rhs_lo) + dot(lhs_lo, rhs_hi))


def swap_blocks(blocks):
    count = len(blocks)
    width = LANES // count
    blocks = list(blocks)
    lane_block = lax.broadcasted_iota(jnp.int32, blocks[0].shape, 1) // width
    half = count // 2
    while half:
        keep = (lane_block & half) == 0
        for i in range(count):
            if i & half == 0:
                low, high = blocks[i], blocks[i + half]
                blocks[i] = jnp.where(keep, low, pltpu.roll(high, half * width, 1))
                blocks[i + half] = jnp.where(
                    keep, pltpu.roll(low, LANES - half * width, 1), high
                )
        half //= 2
    return blocks


def grid_to_time(plane):
    return jnp.concatenate(swap_blocks([plane(i) for i in range(SFT_DEV)]), axis=0)


def owner_dft(real, imag):
    count = len(real)
    if count == 1:
        return real, imag
    half = count // 2
    sum_real = [real[k] + real[k + half] for k in range(half)]
    sum_imag = [imag[k] + imag[k + half] for k in range(half)]
    dif_real, dif_imag = [], []
    for k in range(half):
        d_real, d_imag = real[k] - real[k + half], imag[k] - imag[k + half]
        if k == 0:
            dif_real.append(d_real)
            dif_imag.append(d_imag)
        elif 2 * k == half:
            dif_real.append(d_imag)
            dif_imag.append(-d_real)
        else:
            cos_part = math.cos(2.0 * math.pi * k / count)
            sin_part = math.sin(2.0 * math.pi * k / count)
            dif_real.append(d_real * cos_part + d_imag * sin_part)
            dif_imag.append(d_imag * cos_part - d_real * sin_part)
    even = owner_dft(sum_real, sum_imag)
    odd = owner_dft(dif_real, dif_imag)
    out_real, out_imag = [], []
    for k in range(half):
        out_real += [even[0][k], odd[0][k]]
        out_imag += [even[1][k], odd[1][k]]
    return out_real, out_imag


def search_kernel(
    band_size,
    owners,
    sample_total,
    start_ref,
    bins_ref,
    code_ref,
    ant_ref,
    bins_hi_ref,
    bins_lo_ref,
    bins_twid_ref,
    cols_hi_ref,
    cols_lo_ref,
    left_ref,
    twid_ref,
    right_hi_ref,
    right_lo_ref,
    out_ref,
    grid,
    edge,
    halo,
    buf,
    seg,
    code_t,
    line,
    w_out,
    w_got,
    r_out,
    r_got,
    z_out,
    z_got,
    sums,
    sums_got,
    bin_send,
    bin_recv,
    edge_send,
    edge_recv,
    w_send,
    w_recv,
    s_send,
    s_recv,
    r_send,
    r_recv,
    z_send,
    z_recv,
):
    tmpl_local, grid_rows = code_ref.shape[:2]
    runs = start_ref.shape[1]
    pieces = edge.shape[3]
    per = NQ // SFT_DEV
    block_rows = NQ // owners
    my_tm = lax.axis_index("tm")
    my_band = lax.axis_index("band")
    me = my_tm * band_size + my_band

    def place(rank):
        return {"tm": rank // band_size, "band": rank % band_size}

    def peers(body):
        def step(d, carry):
            body((me + d) % owners)
            return carry

        lax.fori_loop(1, owners, step, 0, unroll=owners <= 8)

    def remote(src, dst, send, recv, rank):
        return pltpu.make_async_remote_copy(
            src_ref=src,
            dst_ref=dst,
            send_sem=send,
            recv_sem=recv,
            device_id=place(rank),
            device_id_type=MESH,
        )

    barrier = pltpu.get_barrier_semaphore()
    peers(
        lambda rank: pl.semaphore_signal(
            barrier, inc=1, device_id=place(rank), device_id_type=MESH
        )
    )

    for e in range(band_size):
        for side in range(2):
            row = SFT_DEV * e + (SFT_DEV - 1 if side == 0 else 0)
            for c in range(2):
                for k in range(pieces):
                    edge[e, side, c, k : k + 1, :] = bins_ref[
                        c, row : row + 1, k * LANES : (k + 1) * LANES
                    ]

    @pl.when(me == 0)
    def _():
        halo[0] = jnp.zeros(halo.shape[1:], jnp.float32)

    @pl.when(me == owners - 1)
    def _():
        halo[1] = jnp.zeros(halo.shape[1:], jnp.float32)

    pl.semaphore_wait(barrier, owners - 1)

    def bins_rows(band):
        return pl.ds(pl.multiple_of(SFT_DEV * band, SFT_DEV), SFT_DEV)

    def bins_copy(d):
        band = (my_band + d) % band_size
        return remote(
            bins_ref.at[:, bins_rows(band), :],
            grid.at[my_band],
            bin_send.at[band],
            bin_recv.at[my_band],
            my_tm * band_size + band,
        )

    def bins_arrival(d):
        band = (my_band + d) % band_size
        return remote(
            bins_ref.at[:, bins_rows(band), :],
            grid.at[band],
            bin_send.at[band],
            bin_recv.at[band],
            my_tm * band_size + band,
        )

    for d in range(1, band_size):
        bins_copy(d).start()

    def edge_target(e, side):
        return my_tm * band_size + e + (1 if side == 0 else -1)

    def edge_copy(e, side):
        return remote(
            edge.at[e, side],
            halo.at[side, my_band],
            edge_send.at[e, side],
            edge_recv.at[side, my_band],
            edge_target(e, side),
        )

    def edge_is_sent(e, side):
        rank = edge_target(e, side)
        return jnp.logical_and(rank != me, jnp.logical_and(rank >= 0, rank < owners))

    for e in range(band_size):
        for side in range(2):

            @pl.when(edge_is_sent(e, side))
            def _():
                edge_copy(e, side).start()

            @pl.when(edge_target(e, side) == me)
            def _():
                halo[side, my_band] = edge[e, side]

    grid[my_band] = bins_ref[:, bins_rows(my_band), :]

    def blocked(value):
        return value.reshape(owners, block_rows, LANES)

    sums[...] = jnp.zeros_like(sums)
    for t in range(tmpl_local):
        wts = []
        for w in range(2):
            value = grid_to_time(lambda i: ant_ref[t, w, pl.ds(i, per, stride=SFT_DEV), :])
            w_out[t, :, w] = blocked(value)
            wts.append(value)
        wa, wb = wts
        for k, product in enumerate((wa * wa, wb * wb, wa * wb)):
            sums[3 * t + k : 3 * t + k + 1, :] = jnp.sum(product, axis=0, keepdims=True)

        def send_w(rank):
            remote(
                w_out.at[t, rank], w_got.at[t, me], w_send.at[t, rank], w_recv.at[t, me], rank
            ).start()

        peers(send_w)
        w_got[t, me] = w_out[t, me]

    peers(
        lambda rank: remote(
            sums, sums_got.at[me], s_send.at[rank], s_recv.at[me], rank
        ).start()
    )
    sums_got[me] = sums[...]

    for t in range(tmpl_local):
        code_t[t] = grid_to_time(lambda i: code_ref[t, pl.ds(i, per, stride=SFT_DEV), :])

    for d in range(1, band_size):
        bins_arrival(d).wait_recv()
    for side in range(2):
        source = (me - 1 if side == 0 else me + 1) // band_size

        @pl.when(jnp.logical_and(me > 0 if side == 0 else me < owners - 1, source != my_tm))
        def _():
            for band in range(band_size):
                remote(
                    edge.at[0, side],
                    halo.at[side, band],
                    edge_send.at[0, side],
                    edge_recv.at[side, band],
                    source * band_size + band,
                ).wait_recv()

        @pl.when(jnp.logical_and(me > 0 if side == 0 else me < owners - 1, source == my_tm))
        def _():
            for d in range(1, band_size):
                band = (my_band + d) % band_size
                remote(
                    edge.at[0, side],
                    halo.at[side, band],
                    edge_send.at[0, side],
                    edge_recv.at[side, band],
                    my_tm * band_size + band,
                ).wait_recv()

    sub = lax.broadcasted_iota(jnp.int32, (SFT_DEV, LANES), 0)
    main_rows, rim_rows = [], []
    for c in range(2):
        for band in range(band_size):
            for k in range(pieces):
                main_rows.append(grid[band, c, :, k * LANES : (k + 1) * LANES])
                first = jnp.broadcast_to(halo[1, band, c, k : k + 1, :], (SFT_DEV, LANES))
                final = jnp.broadcast_to(halo[0, band, c, k : k + 1, :], (SFT_DEV, LANES))
                rim_rows.append(
                    jnp.where(sub == 0, first, jnp.where(sub == SFT_DEV - 1, final, 0.0))
                )
    turned = jnp.concatenate(
        [
            jnp.transpose(jnp.concatenate(main_rows, axis=0)),
            jnp.transpose(jnp.concatenate(rim_rows, axis=0)),
        ],
        axis=0,
    )
    mixed = dot3(split2(turned), (bins_hi_ref[...], bins_lo_ref[...]))
    halves = []
    for h in range(2):
        real = mixed[h * LANES : (h + 1) * LANES, :LANES]
        imag = mixed[h * LANES : (h + 1) * LANES, LANES:]
        cos_part, sin_part = bins_twid_ref[0], bins_twid_ref[1]
        halves.append(
            jnp.concatenate(
                [real * cos_part - imag * sin_part, real * sin_part + imag * cos_part], axis=0
            )
        )
    series = dot3(
        (cols_hi_ref[...], cols_lo_ref[...]), split2(jnp.concatenate(halves, axis=1))
    )
    for c in range(2):
        for h in range(2):
            part = series[c * NQ : (c + 1) * NQ, h * LANES : (h + 1) * LANES]
            blocks = swap_blocks([part[i * per : (i + 1) * per] for i in range(SFT_DEV)])
            if h == 0:
                for s in range(SFT_DEV):
                    buf[pl.ds(2 * per * (s + 1) + c, per, stride=2), :] = blocks[s]
            else:
                buf[pl.ds(c, per, stride=2), :] = blocks[SFT_DEV - 1]
                buf[pl.ds(2 * per * (SFT_DEV + 1) + c, per, stride=2), :] = blocks[0]

    lane = lax.broadcasted_iota(jnp.int32, (8, LANES), 1)
    wide_lane = lax.broadcasted_iota(jnp.int32, (runs, LANES), 1)
    for t in range(tmpl_local):
        for r in range(runs):
            start = start_ref[t, r]
            shift = start & (LANES - 1)
            held = buf[pl.ds(2 * (start >> 7), 8), :]
            rolled = pltpu.roll(held, LANES - shift, 1)
            below = pltpu.roll(rolled, 6, 0)
            seg[8 * r : 8 * r + 8, :] = jnp.where(lane < LANES - shift, rolled, below)
        taps = []
        for c in range(2):
            lines = [seg[pl.ds(2 * r + c, runs, stride=8), :] for r in range(3)]
            moved = [lines] + [
                [pltpu.roll(item, LANES - k, 1) for item in lines] for k in range(1, 4)
            ]
            taps.append(moved)
        for r in range(2):
            code = code_t[t, pl.ds(r, runs, stride=2), :]
            fraction = (code & (NFRAC - 1)).astype(jnp.float32) * (1.0 / NFRAC)
            coeffs = lagrange(fraction)
            for c in range(2):
                moved = taps[c]
                total = coeffs[0] * moved[0][r]
                for k in range(1, 4):
                    total = total + coeffs[k] * jnp.where(
                        wide_lane < LANES - k, moved[k][r], moved[k][r + 1]
                    )
                line[c, pl.ds(r, runs, stride=2), :] = total
        for c in range(2):
            r_out[t, :, c] = blocked(line[c])

        def send_r(rank):
            remote(
                r_out.at[t, rank], r_got.at[t, me], r_send.at[t, rank], r_recv.at[t, me], rank
            ).start()

        peers(send_r)
        r_got[t, me] = r_out[t, me]

    def arrival(out, got, send, recv, t, rank):
        return remote(out.at[t, rank], got.at[t, rank], send.at[t, rank], recv.at[t, rank], rank)

    for t in range(tmpl_local):
        peers(lambda rank: arrival(w_out, w_got, w_send, w_recv, t, rank).wait())
        peers(lambda rank: arrival(r_out, r_got, r_send, r_recv, t, rank).wait())
        for w in range(2):
            real = [r_got[t, i, 0] * w_got[t, i, w] for i in range(owners)]
            imag = [r_got[t, i, 1] * w_got[t, i, w] for i in range(owners)]
            real, imag = owner_dft(real, imag)
            for i in range(owners):
                z_out[t, i, 2 * w] = real[i]
                z_out[t, i, 2 * w + 1] = imag[i]

        def send_z(rank):
            remote(
                z_out.at[t, rank], z_got.at[t, me], z_send.at[t, rank], z_recv.at[t, me], rank
            ).start()

        peers(send_z)
        z_got[t, me] = z_out[t, me]

    def sums_arrival(rank):
        remote(sums, sums_got.at[rank], s_send.at[rank], s_recv.at[rank], rank).wait()

    peers(sums_arrival)
    total = jnp.sum(sums_got[...], axis=0)
    total = jnp.sum(total, axis=1, keepdims=True) / sample_total
    left = split2(left_ref[...])
    norm = 1.0 / math.sqrt(sample_total)
    for t in range(tmpl_local):
        peers(lambda rank: arrival(z_out, z_got, z_send, z_recv, t, rank).wait())
        value = jnp.concatenate(
            [
                jnp.concatenate(
                    [z_got[t, :, 2 * w + c].reshape(NQ, LANES) for c in range(2)], axis=0
                )
                for w in range(2)
            ],
            axis=1,
        )
        mixed = dot3(left, split2(value))
        lines = []
        for w in range(2):
            real = mixed[:NQ, w * LANES : (w + 1) * LANES]
            imag = mixed[NQ:, w * LANES : (w + 1) * LANES]
            cos_part, sin_part = twid_ref[0], twid_ref[1]
            lines.append(
                jnp.concatenate(
                    [real * cos_part - imag * sin_part, real * sin_part + imag * cos_part], axis=1
                )
            )
        spectra = dot3(
            split2(jnp.concatenate(lines, axis=0)), (right_hi_ref[...], right_lo_ref[...])
        ) * norm
        a_real, a_imag = spectra[:NQ, :LANES], spectra[:NQ, LANES:]
        b_real, b_imag = spectra[NQ:, :LANES], spectra[NQ:, LANES:]
        power_a = total[3 * t : 3 * t + 1] + stat_eps
        power_b = total[3 * t + 1 : 3 * t + 2] + stat_eps
        cross_ab = total[3 * t + 2 : 3 * t + 3]
        det = jnp.maximum(
            power_a * power_b - cross_ab * cross_ab, floor_share * power_a * power_b
        )
        stat = (
            power_b * (a_real * a_real + a_imag * a_imag)
            + power_a * (b_real * b_real + b_imag * b_imag)
            - 2.0 * cross_ab * (a_real * b_real + a_imag * b_imag)
        ) / det
        blocks = swap_blocks([stat[i * per : (i + 1) * per] for i in range(SFT_DEV)])
        for j, block in enumerate(blocks):
            out_ref[t, j * per : (j + 1) * per, :] = block

    for d in range(1, band_size):
        bins_copy(d).wait_send()
    for e in range(band_size):
        for side in range(2):

            @pl.when(edge_is_sent(e, side))
            def _():
                edge_copy(e, side).wait_send()


def halves_of(table):
    high = table.astype(ml_dtypes.bfloat16)
    low = (table - high.astype(np.float64)).astype(ml_dtypes.bfloat16)
    return jnp.asarray(high), jnp.asarray(low)


def turns(product, modulus):
    angles = 2.0 * np.pi / modulus * (product % modulus)
    return np.cos(angles), np.sin(angles)


def constant_tables():
    per = NQ // SFT_DEV
    at = np.arange(LANES)
    bin_cos, bin_sin = turns(np.arange(NP)[:, None] * np.arange(NP)[None, :], NP)
    same = np.eye(SFT_DEV)
    wide = [
        np.einsum("kp,st->kstp", part, same).reshape(LANES, LANES) for part in (bin_cos, bin_sin)
    ]
    bins = np.block([[wide[0], wide[1]], [-wide[1], wide[0]]])
    bins_twid = np.stack(turns(at[:, None] * (at % NP)[None, :], NB)).astype(np.float32)
    col_order = at // per + SFT_DEV * (at % per)
    col_cos, col_sin = turns(col_order[:, None] * at[None, :], NQ)
    cols = np.block([[col_cos, -col_sin], [col_sin, col_cos]]) / math.sqrt(NB)
    fine = at // NP + SFT_DEV * (at % NP)
    fine_cos, fine_sin = turns(at[:, None] * fine[None, :], LANES)
    right = np.block([[fine_cos, -fine_sin], [fine_sin, fine_cos]])
    return halves_of(bins) + (jnp.asarray(bins_twid),) + halves_of(cols), halves_of(right)


def per_device(sft_bins, delay_code, antenna):
    band_size = lax.axis_size("band")
    owners = lax.axis_size("tm") * band_size
    sample_total = SFT_DEV * owners * NB
    me = lax.axis_index("tm") * band_size + lax.axis_index("band")
    span_len = SFT_DEV * NB
    tmpl_local = delay_code.shape[0]
    run_count = span_len // RUN
    run_cols = RUN // NP
    offsets = delay_code[:, ::run_cols, ::NP].transpose(0, 2, 1).reshape(tmpl_local, run_count)
    offsets = offsets // NFRAC - MAXD
    starts = (jnp.arange(run_count, dtype=jnp.int32) * RUN)[None, :] + offsets + (NB - 1)
    per = NQ // SFT_DEV
    row_at = lax.broadcasted_iota(jnp.int32, (NQ, LANES), 0)
    col_at = lax.broadcasted_iota(jnp.int32, (NQ, LANES), 1)
    coarse = (row_at // per + SFT_DEV * (row_at % per)) * owners + me
    cos_left, sin_left = phase_pair(coarse * col_at, NQ * owners, -1.0)
    left = jnp.concatenate(
        [
            jnp.concatenate([cos_left, -sin_left], axis=1),
            jnp.concatenate([sin_left, cos_left], axis=1),
        ],
        axis=0,
    )
    twid = jnp.stack(phase_pair(coarse * col_at, sample_total, -1.0))
    first_tables, last_tables = constant_tables()
    vmem = pl.BlockSpec(memory_space=pltpu.VMEM)
    smem = pl.BlockSpec(memory_space=pltpu.SMEM)
    bin_width = sft_bins.shape[2]
    pieces = bin_width // LANES
    block_rows = NQ // owners
    f32 = jnp.float32
    dma = pltpu.SemaphoreType.DMA
    out = pl.pallas_call(
        functools.partial(search_kernel, band_size, owners, sample_total),
        out_shape=jax.ShapeDtypeStruct((tmpl_local, NQ, LANES), f32),
        in_specs=[smem] + [vmem] * 12,
        out_specs=vmem,
        scratch_shapes=[
            pltpu.VMEM((band_size, 2, SFT_DEV, bin_width), f32),
            pltpu.VMEM((band_size, 2, 2, pieces, LANES), f32),
            pltpu.VMEM((2, band_size, 2, pieces, LANES), f32),
            pltpu.VMEM((2 * per * (SFT_DEV + 2), LANES), f32),
            pltpu.VMEM((8 * run_count, LANES), f32),
            pltpu.VMEM((tmpl_local, NQ, LANES), jnp.int32),
            pltpu.VMEM((2, NQ, LANES), f32),
        ]
        + [pltpu.VMEM((tmpl_local, owners, 2, block_rows, LANES), f32)] * 4
        + [pltpu.VMEM((tmpl_local, owners, 4, block_rows, LANES), f32)] * 2
        + [
            pltpu.VMEM((8, LANES), f32),
            pltpu.VMEM((owners, 8, LANES), f32),
            dma((band_size,)),
            dma((band_size,)),
            dma((band_size, 2)),
            dma((2, band_size)),
            dma((tmpl_local, owners)),
            dma((tmpl_local, owners)),
            dma((owners,)),
            dma((owners,)),
        ]
        + [dma((tmpl_local, owners))] * 4,
        compiler_params=pltpu.CompilerParams(
            collective_id=0, has_side_effects=True, vmem_limit_bytes=48 * 1024 * 1024
        ),
    )(starts, sft_bins, delay_code, antenna, *first_tables, left, twid, *last_tables)
    return out[:, :, None, :]


def solution(mesh):
    in_specs = (
        P(None, ("groups", "tm"), "band"),
        P(("groups", "tmpl"), None, ("tm", "band")),
        P(("groups", "tmpl"), None, None, ("tm", "band")),
    )
    out_specs = P(("groups", "tmpl"), None, ("tm", "band"), None)
    return jax.shard_map(
        per_device, mesh=mesh, in_specs=in_specs, out_specs=out_specs, check_vma=False
    )
```

time: 253 us -> 37.7 us (0.15)
  local copies, waits for them, and re-layouts: 181 us -> 4.53 us
  Pallas kernels: 0 us -> 32 us
  blocking collectives: 22.1 us -> 0 us
  starting transfers between devices: 18.9 us -> 0 us
  waiting for transfers between devices: 13.5 us -> 0 us
  matrix products: 10.2 us -> 0 us
  other arithmetic: 4.66 us -> 0.86 us
    gather x384 -> x0, local copies, waits for them, and re-layouts: 169 us -> none
    pallas_call x0 -> x1, Pallas kernels: none -> 32 us  [per_device(): pl.pallas_call(functools.partial(search_kernel, band_size, owners, sample...]
    psum x1 -> x0, blocking collectives: 22.1 us -> none  [per_device(): totals = lax.psum(local_sums, ('tm', 'band'))]
    all_to_all x3 -> x0, starting transfers between devices: 13.6 us -> none  [the longest x1 5.76 us: per_device(): lax.all_to_all(payload[:, :, :, :, None, :], ('tm', 'band'), split_axis=3...]
    all_to_all x3 -> x0, waiting for transfers between devices: 10.3 us -> none  [the longest x1 10.3 us: finish(): lax.all_to_all(packed, ('tm', 'band'), split_axis=4, concat_axis=3, tiled...]
    dot_general x24 -> x0, matrix products: 10.2 us -> none  [the longest x6 2.63 us: complex_einsum(): jnp.einsum(pattern, lhs_imag, rhs_imag, precision=high)]
    ppermute x2 -> x0, starting transfers between devices: 5.31 us -> none  [shifted(): return lax.ppermute(value, axis, pairs)]
    ppermute x2 -> x0, waiting for transfers between devices: 3.2 us -> none  [shifted(): return lax.ppermute(value, axis, pairs)]
  transfers between devices with their start and end apart: 5 -> 0, of which waited for: 2 -> 0; matrix products, arithmetic and copies ran while one was open for 3% -> 0% of each run, Pallas kernels for 0% -> 0%
where the time goes in v2:
time: 37.7 us; the launch traced here: 37.5 us
  Pallas kernels  32 us (85%)
  local copies, waits for them, and re-layouts  4.53 us (12%)
  other arithmetic  0.86 us (2%)
    pallas_call x1, Pallas kernels, per_device(): pl.pallas_call(functools.partial(search_kernel, band_size, owners, sample...  32 us
    unnamed x21, local copies, waits for them, and re-layouts  4.29 us

profile of v2, /device:TPU:0, one launch (start us, length us, event | category | flops | bytes accessed | tf_op | source)
XLA Modules:
  0.0 37.5 jit_solution(807517937506901898)
XLA Ops:
  0.0 0.0 copy-start.5
  0.0 0.0 copy-start.6
  0.0 0.4 %fusion.10 = (f32[128,128]{1,0:T(8,128)S(1)}, f32[128,128]{1,0:T(8,128)S(1)}, f32[128,128]{1,0:T(8,128)S(1)}) fusion(s32[]{:T(128)S(6)} %add.92, s32[128]{0:T(128)S(1)} %get-tuple-element.13, s32[128]{0:T(128)S(1)} %get-tuple-element.14, pred[128]{0:T(512)(128)(4,1)S(1)} %get-tuple-element.10, s32[128]{0:T(128)S(1)} %get-tuple-element.12, ...), kind=kLoop, calls=%fused_computation.18 | loop fusion | flops 344064 | bytes 198916 | tf_op jit(solution)/shard_map/neg | solution.py:536
  0.5 0.0 copy-start.2
  0.5 0.0 copy-start.3
  0.5 0.0 copy-start.4
  0.5 0.0 copy-start
  0.5 0.4 %fusion.7 = (f32[1,128,128]{2,1,0:T(8,128)S(1)}, f32[1,128,128]{2,1,0:T(8,128)S(1)}) fusion(s32[]{:T(128)S(6)} %add.92, s32[128]{0:T(128)S(1)} %get-tuple-element.13, s32[128]{0:T(128)S(1)} %get-tuple-element.14, pred[128]{0:T(512)(128)(4,1)S(1)} %get-tuple-element.10, s32[128]{0:T(128)S(1)} %get-tuple-element.12, s32[128]{0:T(128)S(1)} %get-tuple-element.15, ...), kind=kLoop, calls=%fused_computation.15 | loop fusion | flops 327680 | bytes 133380 | tf_op jit(solution)/shard_map/cos | solution.py:38
  0.9 0.0 copy-start.1
  1.0 0.9 %copy-done.1 = s32[2,128,128]{2,1,0:T(8,128)S(1)} copy-done((s32[2,128,128]{2,1,0:T(8,128)S(1)}, s32[2,128,128]{2,1,0:T(8,128)}, u32[]{:S(2)}) %copy-start.1) | copy-done | bytes 131096
  1.8 0.1 slice.3
  1.9 0.1 copy.11
  2.0 0.1 reshape.286
  2.1 0.0 copy-done.5
  2.1 0.0 copy-done.6
  2.1 0.0 copy-done.2
  2.2 0.0 copy-done.3
  2.2 0.0 copy-done.4
  2.2 0.0 copy-done
  2.2 0.0 copy-start.7
  2.2 0.9 %copy-done.7 = bf16[256,256]{1,0:T(8,128)(2,1)S(1)} copy-done((bf16[256,256]{1,0:T(8,128)(2,1)S(1)}, bf16[256,256]{1,0:T(8,128)(2,1)}, u32[]{:S(2)}) %copy-start.7) | copy-done | bytes 131096
  3.1 0.0 copy-start.8
  3.1 0.9 %copy-done.8 = bf16[256,256]{1,0:T(8,128)(2,1)S(1)} copy-done((bf16[256,256]{1,0:T(8,128)(2,1)S(1)}, bf16[256,256]{1,0:T(8,128)(2,1)}, u32[]{:S(2)}) %copy-start.8) | copy-done | bytes 131096
  4.0 0.0 copy-start.9
  4.0 0.9 %copy-done.9 = bf16[256,256]{1,0:T(8,128)(2,1)S(1)} copy-done((bf16[256,256]{1,0:T(8,128)(2,1)S(1)}, bf16[256,256]{1,0:T(8,128)(2,1)}, u32[]{:S(2)}) %copy-start.9) | copy-done | bytes 131096
  4.9 32.0 %shard_map.100 = f32[2,128,128]{2,1,0:T(8,128)S(1)} custom-call(s32[2,64]{1,0:T(2,128)S(1)} %add_add_fusion.start_ref, f32[2,16,1024]{2,1,0:T(8,128)S(1)} %copy-done.2, s32[2,128,128]{2,1,0:T(8,128)S(1)} %copy-done.1, f32[2,2,128,128]{3,2,1,0:T(8,128)S(1)} %copy-done, bf16[256,256]{1,0:T(8,128)(2,1)S(1)} %copy-done.3, bf16[256,256]{1,0:T(8,128)(2,1)S(1)} %copy-done.4, ...), custom_call_target="tpu_custom_call" | custom-call | tf_op jit(solution)/shard_map/pallas_call | solution.py:550
  36.9 0.7 %copy.14 = f32[2,128,1,128]{3,2,1,0:T(1,128)} copy(f32[2,128,1,128]{3,2,1,0:T(1,128)S(1)} %bitcast.4) | data formatting | bytes 262144
  (7 shorter events, 0.1 us)
Async XLA Ops:
  0.0 2.1 %copy-start.5 = (f32[2,128,128]{2,1,0:T(8,128)S(1)}, f32[2,128,128]{2,1,0:T(8,128)}, u32[]{:S(2)}) copy-start(f32[2,128,128]{2,1,0:T(8,128)} %constant.108.clone.bins_twid_ref) | copy-start | bytes 393220
  0.0 2.1 %copy-start.6 = (bf16[256,256]{1,0:T(8,128)(2,1)S(1)}, bf16[256,256]{1,0:T(8,128)(2,1)}, u32[]{:S(2)}) copy-start(bf16[256,256]{1,0:T(8,128)(2,1)} %constant.109.clone.cols_hi_ref) | copy-start | bytes 393220
  0.5 1.7 %copy-start.2 = (f32[2,16,1024]{2,1,0:T(8,128)S(1)}, f32[2,16,1024]{2,1,0:T(8,128)}, u32[]{:S(2)}) copy-start(f32[2,16,1024]{2,1,0:T(8,128)} %bins_ref.1) | copy-start | bytes 393220
  0.5 1.7 %copy-start.3 = (bf16[256,256]{1,0:T(8,128)(2,1)S(1)}, bf16[256,256]{1,0:T(8,128)(2,1)}, u32[]{:S(2)}) copy-start(bf16[256,256]{1,0:T(8,128)(2,1)} %constant.106.clone.bins_hi_ref) | copy-start | bytes 393220
  0.5 1.7 %copy-start.4 = (bf16[256,256]{1,0:T(8,128)(2,1)S(1)}, bf16[256,256]{1,0:T(8,128)(2,1)}, u32[]{:S(2)}) copy-start(bf16[256,256]{1,0:T(8,128)(2,1)} %constant.107.clone.bins_lo_ref) | copy-start | bytes 393220
  0.5 1.6 %copy-start = (f32[2,2,128,128]{3,2,1,0:T(8,128)S(1)}, f32[2,2,128,128]{3,2,1,0:T(8,128)}, u32[]{:S(2)}) copy-start(f32[2,2,128,128]{3,2,1,0:T(8,128)} %ant_ref.1) | copy-start | bytes 786436
  0.9 0.9 %copy-start.1 = (s32[2,128,128]{2,1,0:T(8,128)S(1)}, s32[2,128,128]{2,1,0:T(8,128)}, u32[]{:S(2)}) copy-start(s32[2,128,128]{2,1,0:T(8,128)} %code_ref.1) | copy-start | bytes 393220
  2.2 0.9 %copy-start.7 = (bf16[256,256]{1,0:T(8,128)(2,1)S(1)}, bf16[256,256]{1,0:T(8,128)(2,1)}, u32[]{:S(2)}) copy-start(bf16[256,256]{1,0:T(8,128)(2,1)} %constant.110.clone.cols_lo_ref) | copy-start | bytes 393220
  3.1 0.9 %copy-start.8 = (bf16[256,256]{1,0:T(8,128)(2,1)S(1)}, bf16[256,256]{1,0:T(8,128)(2,1)}, u32[]{:S(2)}) copy-start(bf16[256,256]{1,0:T(8,128)(2,1)} %constant.111.clone.right_hi_ref) | copy-start | bytes 393220
  4.0 0.9 %copy-start.9 = (bf16[256,256]{1,0:T(8,128)(2,1)S(1)}, bf16[256,256]{1,0:T(8,128)(2,1)}, u32[]{:S(2)}) copy-start(bf16[256,256]{1,0:T(8,128)(2,1)} %constant.112.clone.right_lo_ref) | copy-start | bytes 393220

commit v3 on v2

--- a/solution.py
+++ b/solution.py
@@ -3,7 +3,6 @@
 
 import jax
 import jax.numpy as jnp
-import ml_dtypes
 import numpy as np
 from jax import lax
 from jax.experimental import pallas as pl
@@ -31,11 +30,6 @@
         -(fraction + 1.0) * fraction * (fraction - 2.0) / 2.0,
         (fraction + 1.0) * fraction * (fraction - 1.0) / 6.0,
     )
-
-
-def phase_pair(product, modulus, direction):
-    angles = direction * 2.0 * math.pi / modulus * (product % modulus).astype(jnp.float32)
-    return (jnp.cos(angles), jnp.sin(angles))
 
 
 def split2(value):
@@ -107,20 +101,15 @@
     band_size,
     owners,
     sample_total,
+    far_refs,
+    out_ref,
+    near_refs,
     start_ref,
-    bins_ref,
-    code_ref,
-    ant_ref,
-    bins_hi_ref,
-    bins_lo_ref,
-    bins_twid_ref,
-    cols_hi_ref,
-    cols_lo_ref,
-    left_ref,
-    twid_ref,
-    right_hi_ref,
-    right_lo_ref,
-    out_ref,
+    left_hi,
+    left_lo,
+    right_hi,
+    right_lo,
+    twid,
     grid,
     edge,
     halo,
@@ -148,9 +137,31 @@
     r_recv,
     z_send,
     z_recv,
+    load_sem,
+    start_sem,
 ):
-    tmpl_local, grid_rows = code_ref.shape[:2]
-    runs = start_ref.shape[1]
+    loads = [
+        pltpu.make_async_copy(far, near, load_sem.at[k])
+        for k, (far, near) in enumerate(zip(far_refs, near_refs))
+    ]
+    for load in loads:
+        load.start()
+    (
+        bins_ref,
+        ant_ref,
+        code_ref,
+        bins_table_ref,
+        bins_twid_ref,
+        cols_table_ref,
+        left_ref,
+        twid_ref,
+        right_table_ref,
+    ) = near_refs
+    tmpl_local, run_rows, run_cols, _ = code_ref.shape
+    starts_load = pltpu.make_async_copy(far_refs[2].at[:, :, 0, :], start_ref, start_sem)
+    starts_load.start()
+    runs = SFT_DEV * run_rows
+    code_flat = code_ref.reshape(tmpl_local, NQ, LANES)
     pieces = edge.shape[3]
     per = NQ // SFT_DEV
     block_rows = NQ // owners
@@ -185,6 +196,7 @@
         )
     )
 
+    loads[0].wait()
     for e in range(band_size):
         for side in range(2):
             row = SFT_DEV * e + (SFT_DEV - 1 if side == 0 else 0)
@@ -263,6 +275,7 @@
         return value.reshape(owners, block_rows, LANES)
 
     sums[...] = jnp.zeros_like(sums)
+    loads[1].wait()
     for t in range(tmpl_local):
         wts = []
         for w in range(2):
@@ -288,8 +301,12 @@
     )
     sums_got[me] = sums[...]
 
+    loads[2].wait()
     for t in range(tmpl_local):
-        code_t[t] = grid_to_time(lambda i: code_ref[t, pl.ds(i, per, stride=SFT_DEV), :])
+        code_t[t] = grid_to_time(lambda i: code_flat[t, pl.ds(i, per, stride=SFT_DEV), :])
+    starts_load.wait()
+    for load in loads[3:]:
+        load.wait()
 
     for d in range(1, band_size):
         bins_arrival(d).wait_recv()
@@ -337,7 +354,7 @@
         ],
         axis=0,
     )
-    mixed = dot3(split2(turned), (bins_hi_ref[...], bins_lo_ref[...]))
+    mixed = dot3(split2(turned), split2(bins_table_ref[...]))
     halves = []
     for h in range(2):
         real = mixed[h * LANES : (h + 1) * LANES, :LANES]
@@ -349,7 +366,7 @@
             )
         )
     series = dot3(
-        (cols_hi_ref[...], cols_lo_ref[...]), split2(jnp.concatenate(halves, axis=1))
+        split2(cols_table_ref[...]), split2(jnp.concatenate(halves, axis=1))
     )
     for c in range(2):
         for h in range(2):
@@ -366,7 +383,8 @@
     wide_lane = lax.broadcasted_iota(jnp.int32, (runs, LANES), 1)
     for t in range(tmpl_local):
         for r in range(runs):
-            start = start_ref[t, r]
+            offset = (start_ref[t, r % run_rows, NP * (r // run_rows)] >> 3) - MAXD
+            start = offset + (RUN * r + NB - 1)
             shift = start & (LANES - 1)
             held = buf[pl.ds(2 * (start >> 7), 8), :]
             rolled = pltpu.roll(held, LANES - shift, 1)
@@ -402,6 +420,28 @@
         peers(send_r)
         r_got[t, me] = r_out[t, me]
 
+    at = lax.broadcasted_iota(jnp.int32, (1, LANES), 1) * me
+
+    def advanced(table, modulus):
+        angle = at.astype(jnp.float32) * (2.0 * math.pi / modulus)
+        cos_step, sin_step = jnp.cos(angle), jnp.sin(angle)
+        cos_base, sin_base = table[0], table[1]
+        return (
+            cos_base * cos_step - sin_base * sin_step,
+            sin_base * cos_step + cos_base * sin_step,
+        )
+
+    cos_left, sin_left = advanced(left_ref, NQ * owners)
+    parts = [[cos_left, sin_left], [-sin_left, cos_left]]
+    for i in range(2):
+        for j in range(2):
+            spot = (slice(i * NQ, (i + 1) * NQ), slice(j * NQ, (j + 1) * NQ))
+            left_hi[spot], left_lo[spot] = split2(parts[i][j])
+    right_hi[...], right_lo[...] = split2(right_table_ref[...])
+    cos_part, sin_part = advanced(twid_ref, sample_total)
+    twid[0] = cos_part
+    twid[1] = -sin_part
+
     def arrival(out, got, send, recv, t, rank):
         return remote(out.at[t, rank], got.at[t, rank], send.at[t, rank], recv.at[t, rank], rank)
 
@@ -430,7 +470,6 @@
     peers(sums_arrival)
     total = jnp.sum(sums_got[...], axis=0)
     total = jnp.sum(total, axis=1, keepdims=True) / sample_total
-    left = split2(left_ref[...])
     norm = 1.0 / math.sqrt(sample_total)
     for t in range(tmpl_local):
         peers(lambda rank: arrival(z_out, z_got, z_send, z_recv, t, rank).wait())
@@ -443,19 +482,19 @@
             ],
             axis=1,
         )
-        mixed = dot3(left, split2(value))
+        mixed = dot3((left_hi[...], left_lo[...]), split2(value))
         lines = []
         for w in range(2):
             real = mixed[:NQ, w * LANES : (w + 1) * LANES]
             imag = mixed[NQ:, w * LANES : (w + 1) * LANES]
-            cos_part, sin_part = twid_ref[0], twid_ref[1]
+            cos_part, sin_part = twid[0], twid[1]
             lines.append(
                 jnp.concatenate(
                     [real * cos_part - imag * sin_part, real * sin_part + imag * cos_part], axis=1
                 )
             )
         spectra = dot3(
-            split2(jnp.concatenate(lines, axis=0)), (right_hi_ref[...], right_lo_ref[...])
+            split2(jnp.concatenate(lines, axis=0)), (right_hi[...], right_lo[...])
         ) * norm
         a_real, a_imag = spectra[:NQ, :LANES], spectra[:NQ, LANES:]
         b_real, b_imag = spectra[NQ:, :LANES], spectra[NQ:, LANES:]
@@ -482,12 +521,6 @@
             @pl.when(edge_is_sent(e, side))
             def _():
                 edge_copy(e, side).wait_send()
-
-
-def halves_of(table):
-    high = table.astype(ml_dtypes.bfloat16)
-    low = (table - high.astype(np.float64)).astype(ml_dtypes.bfloat16)
-    return jnp.asarray(high), jnp.asarray(low)
 
 
 def turns(product, modulus):
@@ -504,55 +537,61 @@
         np.einsum("kp,st->kstp", part, same).reshape(LANES, LANES) for part in (bin_cos, bin_sin)
     ]
     bins = np.block([[wide[0], wide[1]], [-wide[1], wide[0]]])
-    bins_twid = np.stack(turns(at[:, None] * (at % NP)[None, :], NB)).astype(np.float32)
+    bins_twid = np.stack(turns(at[:, None] * (at % NP)[None, :], NB))
     col_order = at // per + SFT_DEV * (at % per)
     col_cos, col_sin = turns(col_order[:, None] * at[None, :], NQ)
     cols = np.block([[col_cos, -col_sin], [col_sin, col_cos]]) / math.sqrt(NB)
     fine = at // NP + SFT_DEV * (at % NP)
     fine_cos, fine_sin = turns(at[:, None] * fine[None, :], LANES)
     right = np.block([[fine_cos, -fine_sin], [fine_sin, fine_cos]])
-    return halves_of(bins) + (jnp.asarray(bins_twid),) + halves_of(cols), halves_of(right)
+    left = np.stack(turns(col_order[:, None] * at[None, :], NQ))
+    twid = np.stack(turns(col_order[:, None] * at[None, :], NQ * LANES))
+    tables = (bins, bins_twid, cols, left, twid, right)
+    return tuple(jnp.asarray(table.astype(np.float32)) for table in tables)
 
 
 def per_device(sft_bins, delay_code, antenna):
     band_size = lax.axis_size("band")
     owners = lax.axis_size("tm") * band_size
     sample_total = SFT_DEV * owners * NB
-    me = lax.axis_index("tm") * band_size + lax.axis_index("band")
-    span_len = SFT_DEV * NB
     tmpl_local = delay_code.shape[0]
-    run_count = span_len // RUN
     run_cols = RUN // NP
-    offsets = delay_code[:, ::run_cols, ::NP].transpose(0, 2, 1).reshape(tmpl_local, run_count)
-    offsets = offsets // NFRAC - MAXD
-    starts = (jnp.arange(run_count, dtype=jnp.int32) * RUN)[None, :] + offsets + (NB - 1)
+    runs_down = NQ // run_cols
+    run_count = SFT_DEV * runs_down
     per = NQ // SFT_DEV
-    row_at = lax.broadcasted_iota(jnp.int32, (NQ, LANES), 0)
-    col_at = lax.broadcasted_iota(jnp.int32, (NQ, LANES), 1)
-    coarse = (row_at // per + SFT_DEV * (row_at % per)) * owners + me
-    cos_left, sin_left = phase_pair(coarse * col_at, NQ * owners, -1.0)
-    left = jnp.concatenate(
-        [
-            jnp.concatenate([cos_left, -sin_left], axis=1),
-            jnp.concatenate([sin_left, cos_left], axis=1),
-        ],
-        axis=0,
-    )
-    twid = jnp.stack(phase_pair(coarse * col_at, sample_total, -1.0))
-    first_tables, last_tables = constant_tables()
-    vmem = pl.BlockSpec(memory_space=pltpu.VMEM)
-    smem = pl.BlockSpec(memory_space=pltpu.SMEM)
+    code = delay_code.reshape(tmpl_local, runs_down, run_cols, LANES)
+    operands = (sft_bins, antenna, code) + constant_tables()
     bin_width = sft_bins.shape[2]
     pieces = bin_width // LANES
     block_rows = NQ // owners
     f32 = jnp.float32
     dma = pltpu.SemaphoreType.DMA
+    count = len(operands)
+
+    def kernel(*refs):
+        near = refs[count + 1 : 2 * count + 1]
+        search_kernel(
+            band_size,
+            owners,
+            sample_total,
+            refs[:count],
+            refs[count],
+            near,
+            *refs[2 * count + 1 :],
+        )
+
     out = pl.pallas_call(
-        functools.partial(search_kernel, band_size, owners, sample_total),
+        kernel,
         out_shape=jax.ShapeDtypeStruct((tmpl_local, NQ, LANES), f32),
-        in_specs=[smem] + [vmem] * 12,
-        out_specs=vmem,
-        scratch_shapes=[
+        in_specs=[pl.BlockSpec(memory_space=pl.ANY)] * count,
+        out_specs=pl.BlockSpec(memory_space=pltpu.VMEM),
+        scratch_shapes=[pltpu.VMEM(item.shape, item.dtype) for item in operands]
+        + [
+            pltpu.SMEM((tmpl_local, runs_down, LANES), jnp.int32),
+        ]
+        + [pltpu.VMEM((2 * NQ, 2 * NQ), jnp.bfloat16)] * 4
+        + [
+            pltpu.VMEM((2, NQ, LANES), f32),
             pltpu.VMEM((band_size, 2, SFT_DEV, bin_width), f32),
             pltpu.VMEM((band_size, 2, 2, pieces, LANES), f32),
             pltpu.VMEM((2, band_size, 2, pieces, LANES), f32),
@@ -575,11 +614,12 @@
             dma((owners,)),
             dma((owners,)),
         ]
-        + [dma((tmpl_local, owners))] * 4,
+        + [dma((tmpl_local, owners))] * 4
+        + [dma((count,)), dma],
         compiler_params=pltpu.CompilerParams(
-            collective_id=0, has_side_effects=True, vmem_limit_bytes=48 * 1024 * 1024
+            collective_id=0, has_side_effects=True, vmem_limit_bytes=60 * 1024 * 1024
         ),
-    )(starts, sft_bins, delay_code, antenna, *first_tables, left, twid, *last_tables)
+    )(*operands)
     return out[:, :, None, :]
 
 

time: 37.7 us -> 34 us (0.902)
  local copies, waits for them, and re-layouts: 4.53 us -> 1.57 us
  other arithmetic: 0.86 us -> 0 us
    unnamed x21 -> x1, local copies, waits for them, and re-layouts: 4.29 us -> 1.57 us
    neg x1 -> x0, other arithmetic: 0.41 us -> none  [per_device(): -sin_left]
    cos x1 -> x0, other arithmetic: 0.39 us -> none  [phase_pair(): return (jnp.cos(angles), jnp.sin(angles))]
where the time goes in v3:
time: 34 us; the launch traced here: 33.9 us
  Pallas kernels  32.3 us (95%)
  local copies, waits for them, and re-layouts  1.57 us (5%)
    pallas_call x1, Pallas kernels, per_device(): pl.pallas_call(kernel, out_shape=jax.ShapeDtypeStruct((tmpl_local, NQ, LA...  32.3 us
    unnamed x1, local copies, waits for them, and re-layouts  1.57 us

profile of v3, /device:TPU:0, one launch (start us, length us, event | category | flops | bytes accessed | tf_op | source)
XLA Modules:
  0.0 33.9 jit_solution(778779036764239065)
XLA Ops:
  0.0 32.3 %shard_map.91 = f32[2,128,128]{2,1,0:T(8,128)} custom-call(f32[2,16,1024]{2,1,0:T(8,128)} %refs_0_.1, f32[2,2,128,128]{3,2,1,0:T(8,128)} %refs_1_.1, s32[2,8,16,128]{3,2,1,0:T(8,128)} %bitcast.5, f32[256,256]{1,0:T(8,128)} %constant.12.clone.refs_3_, f32[2,128,128]{2,1,0:T(8,128)} %constant.13.clone.refs_4_, f32[256,256]{1,0:T(8,128)} %constant.14.clone.refs_5_, ...), custom_call_target="tpu_custom_call" | custom-call | tf_op jit(solution)/shard_map/pallas_call | solution.py:583
  32.3 1.6 %copy.12 = f32[2,128,1,128]{3,2,1,0:T(1,128)} copy(f32[2,128,1,128]{3,2,1,0:T(1,128)} %bitcast.4) | data formatting | bytes 262144

commit v4 on v3

--- a/solution.py
+++ b/solution.py
@@ -214,63 +214,6 @@
     def _():
         halo[1] = jnp.zeros(halo.shape[1:], jnp.float32)
 
-    pl.semaphore_wait(barrier, owners - 1)
-
-    def bins_rows(band):
-        return pl.ds(pl.multiple_of(SFT_DEV * band, SFT_DEV), SFT_DEV)
-
-    def bins_copy(d):
-        band = (my_band + d) % band_size
-        return remote(
-            bins_ref.at[:, bins_rows(band), :],
-            grid.at[my_band],
-            bin_send.at[band],
-            bin_recv.at[my_band],
-            my_tm * band_size + band,
-        )
-
-    def bins_arrival(d):
-        band = (my_band + d) % band_size
-        return remote(
-            bins_ref.at[:, bins_rows(band), :],
-            grid.at[band],
-            bin_send.at[band],
-            bin_recv.at[band],
-            my_tm * band_size + band,
-        )
-
-    for d in range(1, band_size):
-        bins_copy(d).start()
-
-    def edge_target(e, side):
-        return my_tm * band_size + e + (1 if side == 0 else -1)
-
-    def edge_copy(e, side):
-        return remote(
-            edge.at[e, side],
-            halo.at[side, my_band],
-            edge_send.at[e, side],
-            edge_recv.at[side, my_band],
-            edge_target(e, side),
-        )
-
-    def edge_is_sent(e, side):
-        rank = edge_target(e, side)
-        return jnp.logical_and(rank != me, jnp.logical_and(rank >= 0, rank < owners))
-
-    for e in range(band_size):
-        for side in range(2):
-
-            @pl.when(edge_is_sent(e, side))
-            def _():
-                edge_copy(e, side).start()
-
-            @pl.when(edge_target(e, side) == me)
-            def _():
-                halo[side, my_band] = edge[e, side]
-
-    grid[my_band] = bins_ref[:, bins_rows(my_band), :]
-
     def blocked(value):
         return value.reshape(owners, block_rows, LANES)
 
@@ -285,6 +228,67 @@
         wa, wb = wts
         for k, product in enumerate((wa * wa, wb * wb, wa * wb)):
             sums[3 * t + k : 3 * t + k + 1, :] = jnp.sum(product, axis=0, keepdims=True)
+        w_got[t, me] = w_out[t, me]
+    sums_got[me] = sums[...]
+
+    pl.semaphore_wait(barrier, owners - 1)
+
+    def bins_rows(band):
+        return pl.ds(pl.multiple_of(SFT_DEV * band, SFT_DEV), SFT_DEV)
+
+    def bins_copy(d):
+        band = (my_band + d) % band_size
+        return remote(
+            bins_ref.at[:, bins_rows(band), :],
+            grid.at[my_band],
+            bin_send.at[band],
+            bin_recv.at[my_band],
+            my_tm * band_size + band,
+        )
+
+    def bins_arrival(d):
+        band = (my_band + d) % band_size
+        return remote(
+            bins_ref.at[:, bins_rows(band), :],
+            grid.at[band],
+            bin_send.at[band],
+            bin_recv.at[band],
+            my_tm * band_size + band,
+        )
+
+    for d in range(1, band_size):
+        bins_copy(d).start()
+
+    def edge_target(e, side):
+        return my_tm * band_size + e + (1 if side == 0 else -1)
+
+    def edge_copy(e, side):
+        return remote(
+            edge.at[e, side],
+            halo.at[side, my_band],
+            edge_send.at[e, side],
+            edge_recv.at[side, my_band],
+            edge_target(e, side),
+        )
+
+    def edge_is_sent(e, side):
+        rank = edge_target(e, side)
+        return jnp.logical_and(rank != me, jnp.logical_and(rank >= 0, rank < owners))
+
+    for e in range(band_size):
+        for side in range(2):
+
+            @pl.when(edge_is_sent(e, side))
+            def _():
+                edge_copy(e, side).start()
+
+            @pl.when(edge_target(e, side) == me)
+            def _():
+                halo[side, my_band] = edge[e, side]
+
+    grid[my_band] = bins_ref[:, bins_rows(my_band), :]
+
+    for t in range(tmpl_local):
 
         def send_w(rank):
             remote(
@@ -292,14 +296,12 @@
             ).start()
 
         peers(send_w)
-        w_got[t, me] = w_out[t, me]
 
     peers(
         lambda rank: remote(
             sums, sums_got.at[me], s_send.at[rank], s_recv.at[me], rank
         ).start()
     )
-    sums_got[me] = sums[...]
 
     loads[2].wait()
     for t in range(tmpl_local):
@@ -560,7 +562,10 @@
     run_count = SFT_DEV * runs_down
     per = NQ // SFT_DEV
     code = delay_code.reshape(tmpl_local, runs_down, run_cols, LANES)
-    operands = (sft_bins, antenna, code) + constant_tables()
+    operands = tuple(
+        pltpu.with_memory_space_constraint(item, pltpu.HBM)
+        for item in (sft_bins, antenna, code) + constant_tables()
+    )
     bin_width = sft_bins.shape[2]
     pieces = bin_width // LANES
     block_rows = NQ // owners
@@ -582,8 +587,8 @@
 
     out = pl.pallas_call(
         kernel,
-        out_shape=jax.ShapeDtypeStruct((tmpl_local, NQ, LANES), f32),
-        in_specs=[pl.BlockSpec(memory_space=pl.ANY)] * count,
+        out_shape=pltpu.VMEM((tmpl_local, NQ, LANES), f32),
+        in_specs=[pl.BlockSpec(memory_space=pltpu.HBM)] * count,
         out_specs=pl.BlockSpec(memory_space=pltpu.VMEM),
         scratch_shapes=[pltpu.VMEM(item.shape, item.dtype) for item in operands]
         + [
@@ -617,7 +622,7 @@
         + [dma((tmpl_local, owners))] * 4
         + [dma((count,)), dma],
         compiler_params=pltpu.CompilerParams(
-            collective_id=0, has_side_effects=True, vmem_limit_bytes=60 * 1024 * 1024
+            collective_id=0, has_side_effects=True, vmem_limit_bytes=48 * 1024 * 1024
         ),
     )(*operands)
     return out[:, :, None, :]

time: 34 us -> 32.3 us (0.950)
  local copies, waits for them, and re-layouts: 1.57 us -> 0.66 us
  Pallas kernels: 32.3 us -> 31.5 us
    unnamed x1, local copies, waits for them, and re-layouts: 1.57 us -> 0.66 us
    pallas_call x1, Pallas kernels: 32.3 us -> 31.5 us  [per_device(): pl.pallas_call(kernel, out_shape=pltpu.VMEM((tmpl_local, NQ, LANES), f32)...]
where the time goes in v4:
time: 32.3 us; the launch traced here: 32.2 us
  Pallas kernels  31.5 us (98%)
  local copies, waits for them, and re-layouts  0.66 us (2%)
    pallas_call x1, Pallas kernels, per_device(): pl.pallas_call(kernel, out_shape=pltpu.VMEM((tmpl_local, NQ, LANES), f32)...  31.5 us
    unnamed x1, local copies, waits for them, and re-layouts  0.66 us

profile of v4, /device:TPU:0, one launch (start us, length us, event | category | flops | bytes accessed | tf_op | source)
XLA Modules:
  0.0 32.2 jit_solution(7859463875242349148)
XLA Ops:
  0.0 31.5 %shard_map.91 = f32[2,128,128]{2,1,0:T(8,128)S(1)} custom-call(f32[2,16,1024]{2,1,0:T(8,128)} %refs_0_.1, f32[2,2,128,128]{3,2,1,0:T(8,128)} %refs_1_.1, s32[2,8,16,128]{3,2,1,0:T(8,128)} %bitcast.5, f32[256,256]{1,0:T(8,128)} %constant.12.clone.refs_3_, f32[2,128,128]{2,1,0:T(8,128)} %constant.13.clone.refs_4_, f32[256,256]{1,0:T(8,128)} %constant.14.clone.refs_5_, ...), custom_call_target="tpu_custom_call" | custom-call | tf_op jit(solution)/shard_map/pallas_call | solution.py:588
  31.5 0.7 %copy.12 = f32[2,128,1,128]{3,2,1,0:T(1,128)} copy(f32[2,128,1,128]{3,2,1,0:T(1,128)S(1)} %bitcast.4) | data formatting | bytes 262144

commit v5 on v4

--- a/solution.py
+++ b/solution.py
@@ -95,6 +95,10 @@
         out_real += [even[0][k], odd[0][k]]
         out_imag += [even[1][k], odd[1][k]]
     return out_real, out_imag
+
+
+def far_first(count):
+    return sorted(range(1, count), key=lambda d: abs(2 * d - count))
 
 
 def search_kernel(
@@ -160,7 +164,6 @@
     tmpl_local, run_rows, run_cols, _ = code_ref.shape
     starts_load = pltpu.make_async_copy(far_refs[2].at[:, :, 0, :], start_ref, start_sem)
     starts_load.start()
-    runs = SFT_DEV * run_rows
     code_flat = code_ref.reshape(tmpl_local, NQ, LANES)
     pieces = edge.shape[3]
     per = NQ // SFT_DEV
@@ -177,7 +180,11 @@
             body((me + d) % owners)
             return carry
 
-        lax.fori_loop(1, owners, step, 0, unroll=owners <= 8)
+        if owners <= SFT_DEV:
+            for d in far_first(owners):
+                body((me + d) % owners)
+        else:
+            lax.fori_loop(1, owners, step, 0)
 
     def remote(src, dst, send, recv, rank):
         return pltpu.make_async_remote_copy(
@@ -305,7 +312,8 @@
 
     loads[2].wait()
     for t in range(tmpl_local):
-        code_t[t] = grid_to_time(lambda i: code_flat[t, pl.ds(i, per, stride=SFT_DEV), :])
+        value = grid_to_time(lambda i: code_flat[t, pl.ds(i, per, stride=SFT_DEV), :])
+        code_t[t] = value.reshape(SFT_DEV, per, LANES)
     starts_load.wait()
     for load in loads[3:]:
         load.wait()
@@ -382,44 +390,59 @@
                 buf[pl.ds(2 * per * (SFT_DEV + 1) + c, per, stride=2), :] = blocks[0]
 
     lane = lax.broadcasted_iota(jnp.int32, (8, LANES), 1)
-    wide_lane = lax.broadcasted_iota(jnp.int32, (runs, LANES), 1)
+    share = owners // SFT_DEV
     for t in range(tmpl_local):
-        for r in range(runs):
-            offset = (start_ref[t, r % run_rows, NP * (r // run_rows)] >> 3) - MAXD
-            start = offset + (RUN * r + NB - 1)
-            shift = start & (LANES - 1)
-            held = buf[pl.ds(2 * (start >> 7), 8), :]
-            rolled = pltpu.roll(held, LANES - shift, 1)
-            below = pltpu.roll(rolled, 6, 0)
-            seg[8 * r : 8 * r + 8, :] = jnp.where(lane < LANES - shift, rolled, below)
-        taps = []
-        for c in range(2):
-            lines = [seg[pl.ds(2 * r + c, runs, stride=8), :] for r in range(3)]
-            moved = [lines] + [
-                [pltpu.roll(item, LANES - k, 1) for item in lines] for k in range(1, 4)
-            ]
-            taps.append(moved)
-        for r in range(2):
-            code = code_t[t, pl.ds(r, runs, stride=2), :]
-            fraction = (code & (NFRAC - 1)).astype(jnp.float32) * (1.0 / NFRAC)
-            coeffs = lagrange(fraction)
+        for d in far_first(SFT_DEV) + [0]:
+            sft = (me // share + d) % SFT_DEV
+            base = d * 8 * run_rows
+            for r in range(run_rows):
+                offset = (start_ref[t, r, NP * sft] >> 3) - MAXD
+                start = offset + (RUN * r + NB - 1) + NB * sft
+                shift = start & (LANES - 1)
+                held = buf[pl.ds(2 * (start >> 7), 8), :]
+                rolled = pltpu.roll(held, LANES - shift, 1)
+                below = pltpu.roll(rolled, 6, 0)
+                seg[base + 8 * r : base + 8 * r + 8, :] = jnp.where(
+                    lane < LANES - shift, rolled, below
+                )
+            coeffs = []
+            for r in range(2):
+                code = code_t[t, sft, pl.ds(r, run_rows, stride=2), :]
+                coeffs.append(
+                    lagrange((code & (NFRAC - 1)).astype(jnp.float32) * (1.0 / NFRAC))
+                )
             for c in range(2):
-                moved = taps[c]
-                total = coeffs[0] * moved[0][r]
-                for k in range(1, 4):
-                    total = total + coeffs[k] * jnp.where(
-                        wide_lane < LANES - k, moved[k][r], moved[k][r + 1]
-                    )
-                line[c, pl.ds(r, runs, stride=2), :] = total
-        for c in range(2):
-            r_out[t, :, c] = blocked(line[c])
-
-        def send_r(rank):
-            remote(
-                r_out.at[t, rank], r_got.at[t, me], r_send.at[t, rank], r_recv.at[t, me], rank
-            ).start()
-
-        peers(send_r)
+                lines = [seg[pl.ds(base + 2 * r + c, run_rows, stride=8), :] for r in range(3)]
+                moved = [lines] + [
+                    [pltpu.roll(item, LANES - k, 1) for item in lines] for k in range(1, 4)
+                ]
+                for r in range(2):
+                    total = coeffs[r][0] * moved[0][r]
+                    for k in range(1, 4):
+                        total = total + coeffs[r][k] * jnp.where(
+                            lane < LANES - k, moved[k][r], moved[k][r + 1]
+                        )
+                    line[d, c, pl.ds(r, run_rows, stride=2), :] = total
+                r_out[t, pl.ds(sft * share, share), c] = line[d, c].reshape(
+                    share, block_rows, LANES
+                )
+
+            def send_r(k, carry):
+                rank = sft * share + k
+
+                @pl.when(rank != me)
+                def _():
+                    remote(
+                        r_out.at[t, rank],
+                        r_got.at[t, me],
+                        r_send.at[t, rank],
+                        r_recv.at[t, me],
+                        rank,
+                    ).start()
+
+                return carry
+
+            lax.fori_loop(0, share, send_r, 0)
         r_got[t, me] = r_out[t, me]
 
     at = lax.broadcasted_iota(jnp.int32, (1, LANES), 1) * me
@@ -602,8 +625,8 @@
             pltpu.VMEM((2, band_size, 2, pieces, LANES), f32),
             pltpu.VMEM((2 * per * (SFT_DEV + 2), LANES), f32),
             pltpu.VMEM((8 * run_count, LANES), f32),
-            pltpu.VMEM((tmpl_local, NQ, LANES), jnp.int32),
-            pltpu.VMEM((2, NQ, LANES), f32),
+            pltpu.VMEM((tmpl_local, SFT_DEV, per, LANES), jnp.int32),
+            pltpu.VMEM((SFT_DEV, 2, per, LANES), f32),
         ]
         + [pltpu.VMEM((tmpl_local, owners, 2, block_rows, LANES), f32)] * 4
         + [pltpu.VMEM((tmpl_local, owners, 4, block_rows, LANES), f32)] * 2

time: 32.3 us -> 34.3 us (1.062)
  Pallas kernels: 31.5 us -> 33.5 us
    pallas_call x1, Pallas kernels: 31.5 us -> 33.5 us  [per_device(): pl.pallas_call(kernel, out_shape=pltpu.VMEM((tmpl_local, NQ, LANES), f32)...]
where the time goes in v5:
time: 34.3 us; the launch traced here: 34.2 us
  Pallas kernels  33.5 us (98%)
  local copies, waits for them, and re-layouts  0.66 us (2%)
    pallas_call x1, Pallas kernels, per_device(): pl.pallas_call(kernel, out_shape=pltpu.VMEM((tmpl_local, NQ, LANES), f32)...  33.5 us

profile of v5, /device:TPU:0, one launch (start us, length us, event | category | flops | bytes accessed | tf_op | source)
XLA Modules:
  0.0 34.2 jit_solution(18363670596594475573)
XLA Ops:
  0.0 33.5 %shard_map.91 = f32[2,128,128]{2,1,0:T(8,128)S(1)} custom-call(f32[2,16,1024]{2,1,0:T(8,128)} %refs_0_.1, f32[2,2,128,128]{3,2,1,0:T(8,128)} %refs_1_.1, s32[2,8,16,128]{3,2,1,0:T(8,128)} %bitcast.5, f32[256,256]{1,0:T(8,128)} %constant.12.clone.refs_3_, f32[2,128,128]{2,1,0:T(8,128)} %constant.13.clone.refs_4_, f32[256,256]{1,0:T(8,128)} %constant.14.clone.refs_5_, ...), custom_call_target="tpu_custom_call" | custom-call | tf_op jit(solution)/shard_map/pallas_call | solution.py:611
  33.5 0.7 %copy.12 = f32[2,128,1,128]{3,2,1,0:T(1,128)} copy(f32[2,128,1,128]{3,2,1,0:T(1,128)S(1)} %bitcast.4) | data formatting | bytes 262144

commit v6 on v5

--- a/solution.py
+++ b/solution.py
@@ -95,10 +95,6 @@
         out_real += [even[0][k], odd[0][k]]
         out_imag += [even[1][k], odd[1][k]]
     return out_real, out_imag
-
-
-def far_first(count):
-    return sorted(range(1, count), key=lambda d: abs(2 * d - count))
 
 
 def search_kernel(
@@ -181,7 +177,7 @@
             return carry
 
         if owners <= SFT_DEV:
-            for d in far_first(owners):
+            for d in range(1, owners):
                 body((me + d) % owners)
         else:
             lax.fori_loop(1, owners, step, 0)
@@ -392,7 +388,7 @@
     lane = lax.broadcasted_iota(jnp.int32, (8, LANES), 1)
     share = owners // SFT_DEV
     for t in range(tmpl_local):
-        for d in far_first(SFT_DEV) + [0]:
+        for d in list(range(1, SFT_DEV)) + [0]:
             sft = (me // share + d) % SFT_DEV
             base = d * 8 * run_rows
             for r in range(run_rows):
@@ -471,8 +467,8 @@
         return remote(out.at[t, rank], got.at[t, rank], send.at[t, rank], recv.at[t, rank], rank)
 
     for t in range(tmpl_local):
-        peers(lambda rank: arrival(w_out, w_got, w_send, w_recv, t, rank).wait())
-        peers(lambda rank: arrival(r_out, r_got, r_send, r_recv, t, rank).wait())
+        peers(lambda rank: arrival(w_out, w_got, w_send, w_recv, t, rank).wait_recv())
+        peers(lambda rank: arrival(r_out, r_got, r_send, r_recv, t, rank).wait_recv())
         for w in range(2):
             real = [r_got[t, i, 0] * w_got[t, i, w] for i in range(owners)]
             imag = [r_got[t, i, 1] * w_got[t, i, w] for i in range(owners)]
@@ -490,14 +486,14 @@
         z_got[t, me] = z_out[t, me]
 
     def sums_arrival(rank):
-        remote(sums, sums_got.at[rank], s_send.at[rank], s_recv.at[rank], rank).wait()
+        remote(sums, sums_got.at[rank], s_send.at[rank], s_recv.at[rank], rank).wait_recv()
 
     peers(sums_arrival)
     total = jnp.sum(sums_got[...], axis=0)
     total = jnp.sum(total, axis=1, keepdims=True) / sample_total
     norm = 1.0 / math.sqrt(sample_total)
     for t in range(tmpl_local):
-        peers(lambda rank: arrival(z_out, z_got, z_send, z_recv, t, rank).wait())
+        peers(lambda rank: arrival(z_out, z_got, z_send, z_recv, t, rank).wait_recv())
         value = jnp.concatenate(
             [
                 jnp.concatenate(
@@ -538,6 +534,14 @@
         for j, block in enumerate(blocks):
             out_ref[t, j * per : (j + 1) * per, :] = block
 
+    def departures(rank):
+        remote(sums, sums_got.at[rank], s_send.at[rank], s_recv.at[rank], rank).wait_send()
+        for t in range(tmpl_local):
+            arrival(w_out, w_got, w_send, w_recv, t, rank).wait_send()
+            arrival(r_out, r_got, r_send, r_recv, t, rank).wait_send()
+            arrival(z_out, z_got, z_send, z_recv, t, rank).wait_send()
+
+    peers(departures)
     for d in range(1, band_size):
         bins_copy(d).wait_send()
     for e in range(band_size):

time: 34.3 us -> 32.4 us (0.945)
  Pallas kernels: 33.5 us -> 31.6 us
    pallas_call x1, Pallas kernels: 33.5 us -> 31.6 us  [per_device(): pl.pallas_call(kernel, out_shape=pltpu.VMEM((tmpl_local, NQ, LANES), f32)...]
where the time goes in v6:
time: 32.4 us; the launch traced here: 32.2 us
  Pallas kernels  31.6 us (98%)
  local copies, waits for them, and re-layouts  0.66 us (2%)
    pallas_call x1, Pallas kernels, per_device(): pl.pallas_call(kernel, out_shape=pltpu.VMEM((tmpl_local, NQ, LANES), f32)...  31.6 us
    unnamed x1, local copies, waits for them, and re-layouts  0.66 us

profile of v6, /device:TPU:0, one launch (start us, length us, event | category | flops | bytes accessed | tf_op | source)
XLA Modules:
  0.0 32.2 jit_solution(8310433454189079277)
XLA Ops:
  0.0 31.6 %shard_map.91 = f32[2,128,128]{2,1,0:T(8,128)S(1)} custom-call(f32[2,16,1024]{2,1,0:T(8,128)} %refs_0_.1, f32[2,2,128,128]{3,2,1,0:T(8,128)} %refs_1_.1, s32[2,8,16,128]{3,2,1,0:T(8,128)} %bitcast.5, f32[256,256]{1,0:T(8,128)} %constant.12.clone.refs_3_, f32[2,128,128]{2,1,0:T(8,128)} %constant.13.clone.refs_4_, f32[256,256]{1,0:T(8,128)} %constant.14.clone.refs_5_, ...), custom_call_target="tpu_custom_call" | custom-call | tf_op jit(solution)/shard_map/pallas_call | solution.py:615
  31.6 0.7 %copy.12 = f32[2,128,1,128]{3,2,1,0:T(1,128)} copy(f32[2,128,1,128]{3,2,1,0:T(1,128)S(1)} %bitcast.4) | data formatting | bytes 262144

commit v7 on v6

--- a/solution.py
+++ b/solution.py
@@ -291,14 +291,18 @@
 
     grid[my_band] = bins_ref[:, bins_rows(my_band), :]
 
-    for t in range(tmpl_local):
-
-        def send_w(rank):
-            remote(
-                w_out.at[t, rank], w_got.at[t, me], w_send.at[t, rank], w_recv.at[t, me], rank
-            ).start()
-
-        peers(send_w)
+    def w_copy(t, w, rank, origin):
+        return remote(
+            w_out.at[t, rank, w],
+            w_got.at[t, origin, w],
+            w_send.at[t, w, rank],
+            w_recv.at[t, w, origin],
+            rank,
+        )
+
+    pairs = [(t, w) for t in range(tmpl_local) for w in range(2)]
+    for t, w in pairs[:-1]:
+        peers(lambda rank: w_copy(t, w, rank, me).start())
 
     peers(
         lambda rank: remote(
@@ -439,6 +443,8 @@
                 return carry
 
             lax.fori_loop(0, share, send_r, 0)
+        if t == 0:
+            peers(lambda rank: w_copy(*pairs[-1], rank, me).start())
         r_got[t, me] = r_out[t, me]
 
     at = lax.broadcasted_iota(jnp.int32, (1, LANES), 1) * me
@@ -458,7 +464,7 @@
         for j in range(2):
             spot = (slice(i * NQ, (i + 1) * NQ), slice(j * NQ, (j + 1) * NQ))
             left_hi[spot], left_lo[spot] = split2(parts[i][j])
-    right_hi[...], right_lo[...] = split2(right_table_ref[...])
+    right_hi[...], right_lo[...] = split2(right_table_ref[...] * (1.0 / math.sqrt(sample_total)))
     cos_part, sin_part = advanced(twid_ref, sample_total)
     twid[0] = cos_part
     twid[1] = -sin_part
@@ -467,7 +473,8 @@
         return remote(out.at[t, rank], got.at[t, rank], send.at[t, rank], recv.at[t, rank], rank)
 
     for t in range(tmpl_local):
-        peers(lambda rank: arrival(w_out, w_got, w_send, w_recv, t, rank).wait_recv())
+        for w in range(2):
+            peers(lambda rank: w_copy(t, w, rank, rank).wait_recv())
         peers(lambda rank: arrival(r_out, r_got, r_send, r_recv, t, rank).wait_recv())
         for w in range(2):
             real = [r_got[t, i, 0] * w_got[t, i, w] for i in range(owners)]
@@ -491,7 +498,6 @@
     peers(sums_arrival)
     total = jnp.sum(sums_got[...], axis=0)
     total = jnp.sum(total, axis=1, keepdims=True) / sample_total
-    norm = 1.0 / math.sqrt(sample_total)
     for t in range(tmpl_local):
         peers(lambda rank: arrival(z_out, z_got, z_send, z_recv, t, rank).wait_recv())
         value = jnp.concatenate(
@@ -516,7 +522,7 @@
             )
         spectra = dot3(
             split2(jnp.concatenate(lines, axis=0)), (right_hi[...], right_lo[...])
-        ) * norm
+        )
         a_real, a_imag = spectra[:NQ, :LANES], spectra[:NQ, LANES:]
         b_real, b_imag = spectra[NQ:, :LANES], spectra[NQ:, LANES:]
         power_a = total[3 * t : 3 * t + 1] + stat_eps
@@ -526,10 +532,10 @@
             power_a * power_b - cross_ab * cross_ab, floor_share * power_a * power_b
         )
         stat = (
-            power_b * (a_real * a_real + a_imag * a_imag)
-            + power_a * (b_real * b_real + b_imag * b_imag)
-            - 2.0 * cross_ab * (a_real * b_real + a_imag * b_imag)
-        ) / det
+            (power_b / det) * (a_real * a_real + a_imag * a_imag)
+            + (power_a / det) * (b_real * b_real + b_imag * b_imag)
+            - (2.0 * cross_ab / det) * (a_real * b_real + a_imag * b_imag)
+        )
         blocks = swap_blocks([stat[i * per : (i + 1) * per] for i in range(SFT_DEV)])
         for j, block in enumerate(blocks):
             out_ref[t, j * per : (j + 1) * per, :] = block
@@ -537,7 +543,8 @@
     def departures(rank):
         remote(sums, sums_got.at[rank], s_send.at[rank], s_recv.at[rank], rank).wait_send()
         for t in range(tmpl_local):
-            arrival(w_out, w_got, w_send, w_recv, t, rank).wait_send()
+            for w in range(2):
+                w_copy(t, w, rank, rank).wait_send()
             arrival(r_out, r_got, r_send, r_recv, t, rank).wait_send()
             arrival(z_out, z_got, z_send, z_recv, t, rank).wait_send()
 
@@ -641,8 +648,8 @@
             dma((band_size,)),
             dma((band_size, 2)),
             dma((2, band_size)),
-            dma((tmpl_local, owners)),
-            dma((tmpl_local, owners)),
+            dma((tmpl_local, 2, owners)),
+            dma((tmpl_local, 2, owners)),
             dma((owners,)),
             dma((owners,)),
         ]

time: 32.4 us -> 32.6 us (level)
  no operation moved by 1% of the time
where the time goes in v7:
time: 32.6 us; the launch traced here: 32.4 us
  Pallas kernels  31.7 us (97%)
  local copies, waits for them, and re-layouts  0.66 us (2%)
    pallas_call x1, Pallas kernels, per_device(): pl.pallas_call(kernel, out_shape=pltpu.VMEM((tmpl_local, NQ, LANES), f32)...  31.7 us
    unnamed x1, local copies, waits for them, and re-layouts  0.66 us

profile of v7, /device:TPU:0, one launch (start us, length us, event | category | flops | bytes accessed | tf_op | source)
XLA Modules:
  0.0 32.4 jit_solution(879074903839596637)
XLA Ops:
  0.0 31.7 %shard_map.91 = f32[2,128,128]{2,1,0:T(8,128)S(1)} custom-call(f32[2,16,1024]{2,1,0:T(8,128)} %refs_0_.1, f32[2,2,128,128]{3,2,1,0:T(8,128)} %refs_1_.1, s32[2,8,16,128]{3,2,1,0:T(8,128)} %bitcast.5, f32[256,256]{1,0:T(8,128)} %constant.12.clone.refs_3_, f32[2,128,128]{2,1,0:T(8,128)} %constant.13.clone.refs_4_, f32[256,256]{1,0:T(8,128)} %constant.14.clone.refs_5_, ...), custom_call_target="tpu_custom_call" | custom-call | tf_op jit(solution)/shard_map/pallas_call | solution.py:622
  31.8 0.7 %copy.12 = f32[2,128,1,128]{3,2,1,0:T(1,128)} copy(f32[2,128,1,128]{3,2,1,0:T(1,128)S(1)} %bitcast.4) | data formatting | bytes 262144

commit v8 on v7

--- a/solution.py
+++ b/solution.py
@@ -109,6 +109,10 @@
     left_lo,
     right_hi,
     right_lo,
+    bins_hi,
+    bins_lo,
+    cols_hi,
+    cols_lo,
     twid,
     grid,
     edge,
@@ -220,6 +224,63 @@
     def blocked(value):
         return value.reshape(owners, block_rows, LANES)
 
+    pl.semaphore_wait(barrier, owners - 1)
+
+    def bins_rows(band):
+        return pl.ds(pl.multiple_of(SFT_DEV * band, SFT_DEV), SFT_DEV)
+
+    def bins_copy(d):
+        band = (my_band + d) % band_size
+        return remote(
+            bins_ref.at[:, bins_rows(band), :],
+            grid.at[my_band],
+            bin_send.at[band],
+            bin_recv.at[my_band],
+            my_tm * band_size + band,
+        )
+
+    def bins_arrival(d):
+        band = (my_band + d) % band_size
+        return remote(
+            bins_ref.at[:, bins_rows(band), :],
+            grid.at[band],
+            bin_send.at[band],
+            bin_recv.at[band],
+            my_tm * band_size + band,
+        )
+
+    for d in range(1, band_size):
+        bins_copy(d).start()
+
+    def edge_target(e, side):
+        return my_tm * band_size + e + (1 if side == 0 else -1)
+
+    def edge_copy(e, side):
+        return remote(
+            edge.at[e, side],
+            halo.at[side, my_band],
+            edge_send.at[e, side],
+            edge_recv.at[side, my_band],
+            edge_target(e, side),
+        )
+
+    def edge_is_sent(e, side):
+        rank = edge_target(e, side)
+        return jnp.logical_and(rank != me, jnp.logical_and(rank >= 0, rank < owners))
+
+    for e in range(band_size):
+        for side in range(2):
+
+            @pl.when(edge_is_sent(e, side))
+            def _():
+                edge_copy(e, side).start()
+
+            @pl.when(edge_target(e, side) == me)
+            def _():
+                halo[side, my_band] = edge[e, side]
+
+    grid[my_band] = bins_ref[:, bins_rows(my_band), :]
+
     sums[...] = jnp.zeros_like(sums)
     loads[1].wait()
     for t in range(tmpl_local):
@@ -234,63 +295,6 @@
         w_got[t, me] = w_out[t, me]
     sums_got[me] = sums[...]
 
-    pl.semaphore_wait(barrier, owners - 1)
-
-    def bins_rows(band):
-        return pl.ds(pl.multiple_of(SFT_DEV * band, SFT_DEV), SFT_DEV)
-
-    def bins_copy(d):
-        band = (my_band + d) % band_size
-        return remote(
-            bins_ref.at[:, bins_rows(band), :],
-            grid.at[my_band],
-            bin_send.at[band],
-            bin_recv.at[my_band],
-            my_tm * band_size + band,
-        )
-
-    def bins_arrival(d):
-        band = (my_band + d) % band_size
-        return remote(
-            bins_ref.at[:, bins_rows(band), :],
-            grid.at[band],
-            bin_send.at[band],
-            bin_recv.at[band],
-            my_tm * band_size + band,
-        )
-
-    for d in range(1, band_size):
-        bins_copy(d).start()
-
-    def edge_target(e, side):
-        return my_tm * band_size + e + (1 if side == 0 else -1)
-
-    def edge_copy(e, side):
-        return remote(
-            edge.at[e, side],
-            halo.at[side, my_band],
-            edge_send.at[e, side],
-            edge_recv.at[side, my_band],
-            edge_target(e, side),
-        )
-
-    def edge_is_sent(e, side):
-        rank = edge_target(e, side)
-        return jnp.logical_and(rank != me, jnp.logical_and(rank >= 0, rank < owners))
-
-    for e in range(band_size):
-        for side in range(2):
-
-            @pl.when(edge_is_sent(e, side))
-            def _():
-                edge_copy(e, side).start()
-
-            @pl.when(edge_target(e, side) == me)
-            def _():
-                halo[side, my_band] = edge[e, side]
-
-    grid[my_band] = bins_ref[:, bins_rows(my_band), :]
-
     def w_copy(t, w, rank, origin):
         return remote(
             w_out.at[t, rank, w],
@@ -301,7 +305,7 @@
         )
 
     pairs = [(t, w) for t in range(tmpl_local) for w in range(2)]
-    for t, w in pairs[:-1]:
+    for t, w in pairs[:2]:
         peers(lambda rank: w_copy(t, w, rank, me).start())
 
     peers(
@@ -317,6 +321,9 @@
     starts_load.wait()
     for load in loads[3:]:
         load.wait()
+    bins_hi[...], bins_lo[...] = split2(bins_table_ref[...])
+    cols_hi[...], cols_lo[...] = split2(cols_table_ref[...])
+    right_hi[...], right_lo[...] = split2(right_table_ref[...] * (1.0 / math.sqrt(sample_total)))
 
     for d in range(1, band_size):
         bins_arrival(d).wait_recv()
@@ -346,6 +353,8 @@
                     my_tm * band_size + band,
                 ).wait_recv()
 
+    for t, w in pairs[2:]:
+        peers(lambda rank: w_copy(t, w, rank, me).start())
     sub = lax.broadcasted_iota(jnp.int32, (SFT_DEV, LANES), 0)
     main_rows, rim_rows = [], []
     for c in range(2):
@@ -364,7 +373,7 @@
         ],
         axis=0,
     )
-    mixed = dot3(split2(turned), split2(bins_table_ref[...]))
+    mixed = dot3(split2(turned), (bins_hi[...], bins_lo[...]))
     halves = []
     for h in range(2):
         real = mixed[h * LANES : (h + 1) * LANES, :LANES]
@@ -376,7 +385,7 @@
             )
         )
     series = dot3(
-        split2(cols_table_ref[...]), split2(jnp.concatenate(halves, axis=1))
+        (cols_hi[...], cols_lo[...]), split2(jnp.concatenate(halves, axis=1))
     )
     for c in range(2):
         for h in range(2):
@@ -443,8 +452,6 @@
                 return carry
 
             lax.fori_loop(0, share, send_r, 0)
-        if t == 0:
-            peers(lambda rank: w_copy(*pairs[-1], rank, me).start())
         r_got[t, me] = r_out[t, me]
 
     at = lax.broadcasted_iota(jnp.int32, (1, LANES), 1) * me
@@ -464,7 +471,6 @@
         for j in range(2):
             spot = (slice(i * NQ, (i + 1) * NQ), slice(j * NQ, (j + 1) * NQ))
             left_hi[spot], left_lo[spot] = split2(parts[i][j])
-    right_hi[...], right_lo[...] = split2(right_table_ref[...] * (1.0 / math.sqrt(sample_total)))
     cos_part, sin_part = advanced(twid_ref, sample_total)
     twid[0] = cos_part
     twid[1] = -sin_part
@@ -628,7 +634,7 @@
         + [
             pltpu.SMEM((tmpl_local, runs_down, LANES), jnp.int32),
         ]
-        + [pltpu.VMEM((2 * NQ, 2 * NQ), jnp.bfloat16)] * 4
+        + [pltpu.VMEM((2 * NQ, 2 * NQ), jnp.bfloat16)] * 8
         + [
             pltpu.VMEM((2, NQ, LANES), f32),
             pltpu.VMEM((band_size, 2, SFT_DEV, bin_width), f32),

time: 32.6 us -> 33.4 us (1.025)
  Pallas kernels: 31.7 us -> 32.6 us
    pallas_call x1, Pallas kernels: 31.7 us -> 32.6 us  [per_device(): pl.pallas_call(kernel, out_shape=pltpu.VMEM((tmpl_local, NQ, LANES), f32)...]
where the time goes in v8:
time: 33.4 us; the launch traced here: 33.2 us
  Pallas kernels  32.6 us (98%)
  local copies, waits for them, and re-layouts  0.66 us (2%)
    pallas_call x1, Pallas kernels, per_device(): pl.pallas_call(kernel, out_shape=pltpu.VMEM((tmpl_local, NQ, LANES), f32)...  32.6 us

profile of v8, /device:TPU:0, one launch (start us, length us, event | category | flops | bytes accessed | tf_op | source)
XLA Modules:
  0.0 33.2 jit_solution(255029467426164827)
XLA Ops:
  0.0 32.6 %shard_map.91 = f32[2,128,128]{2,1,0:T(8,128)S(1)} custom-call(f32[2,16,1024]{2,1,0:T(8,128)} %refs_0_.1, f32[2,2,128,128]{3,2,1,0:T(8,128)} %refs_1_.1, s32[2,8,16,128]{3,2,1,0:T(8,128)} %bitcast.5, f32[256,256]{1,0:T(8,128)} %constant.12.clone.refs_3_, f32[2,128,128]{2,1,0:T(8,128)} %constant.13.clone.refs_4_, f32[256,256]{1,0:T(8,128)} %constant.14.clone.refs_5_, ...), custom_call_target="tpu_custom_call" | custom-call | tf_op jit(solution)/shard_map/pallas_call | solution.py:628
  32.6 0.7 %copy.12 = f32[2,128,1,128]{3,2,1,0:T(1,128)} copy(f32[2,128,1,128]{3,2,1,0:T(1,128)S(1)} %bitcast.4) | data formatting | bytes 262144

commit v9 on v7

--- a/solution.py
+++ b/solution.py
@@ -109,6 +109,10 @@
     left_lo,
     right_hi,
     right_lo,
+    bins_hi,
+    bins_lo,
+    cols_hi,
+    cols_lo,
     twid,
     grid,
     edge,
@@ -301,7 +305,7 @@
         )
 
     pairs = [(t, w) for t in range(tmpl_local) for w in range(2)]
-    for t, w in pairs[:-1]:
+    for t, w in pairs:
         peers(lambda rank: w_copy(t, w, rank, me).start())
 
     peers(
@@ -317,6 +321,8 @@
     starts_load.wait()
     for load in loads[3:]:
         load.wait()
+    bins_hi[...], bins_lo[...] = split2(bins_table_ref[...])
+    cols_hi[...], cols_lo[...] = split2(cols_table_ref[...])
 
     for d in range(1, band_size):
         bins_arrival(d).wait_recv()
@@ -364,7 +370,7 @@
         ],
         axis=0,
     )
-    mixed = dot3(split2(turned), split2(bins_table_ref[...]))
+    mixed = dot3(split2(turned), (bins_hi[...], bins_lo[...]))
     halves = []
     for h in range(2):
         real = mixed[h * LANES : (h + 1) * LANES, :LANES]
@@ -376,7 +382,7 @@
             )
         )
     series = dot3(
-        split2(cols_table_ref[...]), split2(jnp.concatenate(halves, axis=1))
+        (cols_hi[...], cols_lo[...]), split2(jnp.concatenate(halves, axis=1))
     )
     for c in range(2):
         for h in range(2):
@@ -443,8 +449,6 @@
                 return carry
 
             lax.fori_loop(0, share, send_r, 0)
-        if t == 0:
-            peers(lambda rank: w_copy(*pairs[-1], rank, me).start())
         r_got[t, me] = r_out[t, me]
 
     at = lax.broadcasted_iota(jnp.int32, (1, LANES), 1) * me
@@ -628,7 +632,7 @@
         + [
             pltpu.SMEM((tmpl_local, runs_down, LANES), jnp.int32),
         ]
-        + [pltpu.VMEM((2 * NQ, 2 * NQ), jnp.bfloat16)] * 4
+        + [pltpu.VMEM((2 * NQ, 2 * NQ), jnp.bfloat16)] * 8
         + [
             pltpu.VMEM((2, NQ, LANES), f32),
             pltpu.VMEM((band_size, 2, SFT_DEV, bin_width), f32),

time: 32.6 us -> 32.6 us (level)
  no operation moved by 1% of the time
where the time goes in v9:
time: 32.6 us; the launch traced here: 32.5 us
  Pallas kernels  31.8 us (98%)
  local copies, waits for them, and re-layouts  0.66 us (2%)
    pallas_call x1, Pallas kernels, per_device(): pl.pallas_call(kernel, out_shape=pltpu.VMEM((tmpl_local, NQ, LANES), f32)...  31.8 us
    unnamed x1, local copies, waits for them, and re-layouts  0.66 us

profile of v9, /device:TPU:0, one launch (start us, length us, event | category | flops | bytes accessed | tf_op | source)
XLA Modules:
  0.0 32.5 jit_solution(5438336150307024396)
XLA Ops:
  0.0 31.8 %shard_map.91 = f32[2,128,128]{2,1,0:T(8,128)S(1)} custom-call(f32[2,16,1024]{2,1,0:T(8,128)} %refs_0_.1, f32[2,2,128,128]{3,2,1,0:T(8,128)} %refs_1_.1, s32[2,8,16,128]{3,2,1,0:T(8,128)} %bitcast.5, f32[256,256]{1,0:T(8,128)} %constant.12.clone.refs_3_, f32[2,128,128]{2,1,0:T(8,128)} %constant.13.clone.refs_4_, f32[256,256]{1,0:T(8,128)} %constant.14.clone.refs_5_, ...), custom_call_target="tpu_custom_call" | custom-call | tf_op jit(solution)/shard_map/pallas_call | solution.py:626
  31.8 0.7 %copy.12 = f32[2,128,1,128]{3,2,1,0:T(1,128)} copy(f32[2,128,1,128]{3,2,1,0:T(1,128)S(1)} %bitcast.4) | data formatting | bytes 262144
